TPU v7x, 128 devices: a whole 4x4x4 slice. The times are simulated.
128 devices in a mesh: region: 128 (over z, x, y, core).
Axes of the slice: x: 4, y: 4, z: 4, core: 2. Of those that a mesh axis runs over, the one named last changes fastest.
Arguments:
- gaussians: float32 [128, 9, 4096], P('region')
- depth: int32 [128, 512, 8], P('region'), may hold values from 0 to 7, each once within a row
- coverage: int32 [128, 512], P('region'), may hold values 0 or 1
- flips: int32 [512, 127], replicated, may hold values 0 or 1
- features: bfloat16 [131072, 384], P('region'), may hold values from -6 to 6
- w_first: bfloat16 [384, 384], replicated, may hold values from -0.3125 to 0.3125
- b_first: float32 [384], replicated, may hold values from -3 to 3
- w_second: bfloat16 [384], replicated, may hold values from -0.3125 to 0.3125
- target: float32 [3, 131072], P(None, 'region'), may hold values from 0 to 1
Outputs:
- pixel_loss: float32 [131072], P('region')
- splat_grads: float32 [128, 9, 4096], P('region')
Inputs may be any that keep to these rules, and one draw needn't show every extreme that they name: Each tile's 8 depth ranks of one region are a permutation of 0 to 7.
All inputs are finite; a program needn't handle non-finite values. No bound on the sum of `coverage` on one device may be relied on, other than what follows from the above.
Results may differ from a plain program's by a relative error of at most 0.0022.
Values sent between devices are 32-bit elements; how exact they have to be, the bound alone decides.
No kernel may reach another device: no remote copies, remote signals or barrier semaphores. Data moves between devices by JAX's collectives and lax.ppermute only.
A program may use at most 64 MiB of HBM per device.

v0:
```python
import jax
import jax.numpy as jnp
from jax import lax
from jax.sharding import PartitionSpec as P

TSIDE = 16


def render_tiles(params, splat_ranks, covered):
    pixel_index = jnp.arange(TSIDE * TSIDE)
    column_pos = (pixel_index % TSIDE).astype(jnp.float32) + 0.5
    row_pos = (pixel_index // TSIDE).astype(jnp.float32) + 0.5
    delta_x = column_pos[None, None, :] - params[0][:, :, None]
    delta_y = row_pos[None, None, :] - params[1][:, :, None]
    unit_x = delta_x * jnp.exp(-params[2])[:, :, None]
    unit_y = delta_y * jnp.exp(-params[3])[:, :, None]
    correlation = (0.9 * jnp.tanh(params[4]))[:, :, None]
    quadratic = (unit_x * unit_x - 2.0 * correlation * unit_x * unit_y + unit_y * unit_y) / (
        1.0 - correlation * correlation
    )
    opacity = 0.99 * jax.nn.sigmoid(params[5]) * covered[:, None].astype(jnp.float32)
    absorb = opacity[:, :, None] * jnp.exp(-0.5 * quadratic)
    log_trans = jnp.log1p(-absorb)
    prior = (splat_ranks[:, None, :] < splat_ranks[:, :, None]).astype(jnp.float32)
    leading = jnp.einsum("tgh,thp->tgp", prior, log_trans, precision=lax.Precision.HIGHEST)
    weight = jnp.exp(leading) * absorb
    colors = jax.nn.sigmoid(params[6:9])
    color_sum = jnp.sum(colors[:, :, :, None] * weight[None], 2)
    transmit = jnp.exp(jnp.sum(log_trans, axis=1))
    return jnp.concatenate([color_sum, transmit[None]], 0)


def over_pair(front_layer, back_layer):
    blended = front_layer[:, :3] + front_layer[:, 3:4] * back_layer[:, :3]
    transmit = front_layer[:, 3:4] * back_layer[:, 3:4]
    return jnp.concatenate([blended, transmit], 1)


def adjoint_pair(gradient, front_layer, back_layer, in_front):
    grad_color = gradient[:, :3]
    grad_trans = gradient[:, 3:4]
    front_grad = jnp.concatenate(
        [
            grad_color,
            jnp.sum(grad_color * back_layer[:, :3], 1, keepdims=True)
            + grad_trans * back_layer[:, 3:4],
        ],
        1,
    )
    back_grad = jnp.concatenate(
        [front_layer[:, 3:4] * grad_color, grad_trans * front_layer[:, 3:4]], 1
    )
    return (jnp.where(in_front, back_grad, front_grad), jnp.where(in_front, front_grad, back_grad))


def tree_levels(stack, stripe_flips):
    stored = []
    number = stack.shape[0]
    while number > 1:
        half_count = number // 2
        in_front = (stripe_flips[:, half_count - 1 : 2 * half_count - 1].T > 0)[:, None, :, None]
        paired = stack.reshape((half_count, 2) + stack.shape[1:])
        front_layer = jnp.where(in_front, paired[:, 1], paired[:, 0])
        back_layer = jnp.where(in_front, paired[:, 0], paired[:, 1])
        stored.append((front_layer, back_layer, in_front))
        stack = over_pair(front_layer, back_layer)
        number = half_count
    return (stack[0], stored)


def tree_adjoint(gradient, stored):
    for front_layer, back_layer, in_front in reversed(stored):
        low_half, high_half = adjoint_pair(gradient, front_layer, back_layer, in_front)
        gradient = jnp.stack([low_half, high_half], 1).reshape(
            (2 * low_half.shape[0],) + low_half.shape[1:]
        )
    return gradient


def uncertainty(stripe_feats, w_first, b_first, w_second):
    hidden = jax.nn.gelu(
        jnp.dot(stripe_feats, w_first, preferred_element_type=jnp.float32) + b_first
    ).astype(jnp.bfloat16)
    return 0.5 + jax.nn.softplus(jnp.dot(hidden, w_second, preferred_element_type=jnp.float32))


def loss_gradient(composite, wanted, spread):
    residual = composite[:3] + composite[3:4] - wanted
    inv_square = 1.0 / (spread * spread)
    pixel_loss = 0.5 * jnp.sum(residual * residual, 0) * inv_square + jnp.log(spread)
    grad_color = residual * inv_square
    return (pixel_loss, jnp.concatenate([grad_color, jnp.sum(grad_color, 0, keepdims=True)], 0))


def shards(gaussians, depth, coverage, flips, features, w_first, b_first, w_second, target):
    regions = lax.axis_size("region")
    my_index = lax.axis_index("region")
    tile_count = depth.shape[1]
    splats = depth.shape[2]
    stripe_tiles = tile_count // regions
    tile_pixels = TSIDE * TSIDE
    block_size = 64
    block_count = tile_count // block_size
    params = gaussians[0].reshape(9, tile_count, splats)
    param_blocks = params.reshape(9, block_count, block_size, splats).transpose(1, 0, 2, 3)
    rank_blocks = depth[0].reshape(block_count, block_size, splats)
    cover_blocks = coverage[0].reshape(block_count, block_size)

    def render_block(inputs):
        return render_tiles(inputs[0], inputs[1], inputs[2])

    partial_value = lax.map(render_block, (param_blocks, rank_blocks, cover_blocks))
    partial_value = partial_value.transpose(1, 0, 2, 3).reshape(4, tile_count, tile_pixels)
    spread = uncertainty(features, w_first, b_first, w_second).reshape(stripe_tiles, tile_pixels)
    wanted = target.reshape(3, stripe_tiles, tile_pixels)
    pieces = lax.all_to_all(partial_value[None], "region", split_axis=2, concat_axis=0, tiled=True)
    my_flips = lax.dynamic_slice_in_dim(flips, my_index * stripe_tiles, stripe_tiles, 0)
    composite, stored = tree_levels(pieces, my_flips)
    pixel_loss, grad_whole = loss_gradient(composite, wanted, spread)
    adjoint = tree_adjoint(grad_whole[None], stored)
    returned = lax.all_to_all(adjoint, "region", split_axis=0, concat_axis=2, tiled=True)
    cotangent = returned[0]
    cotangent_blocks = cotangent.reshape(4, block_count, block_size, tile_pixels).transpose(
        1, 0, 2, 3
    )

    def pull_block(inputs):
        block_params, block_ranks, block_cover, block_cotangent = inputs

        def local_render(given_params):
            return render_tiles(given_params, block_ranks, block_cover)

        unused_out, pull_back = jax.vjp(local_render, block_params)
        return pull_back(block_cotangent)[0]

    gradients = lax.map(pull_block, (param_blocks, rank_blocks, cover_blocks, cotangent_blocks))
    splat_grads = gradients.transpose(1, 0, 2, 3).reshape(1, 9, tile_count * splats)
    return (pixel_loss.reshape(stripe_tiles * tile_pixels), splat_grads)


def solution(mesh):
    placed = (
        P("region", None, None),
        P("region", None, None),
        P("region", None),
        P(),
        P("region", None),
        P(),
        P(),
        P(),
        P(None, "region"),
    )
    return jax.shard_map(
        shards,
        mesh=mesh,
        in_specs=placed,
        out_specs=(P("region"), P("region", None, None)),
        check_vma=False,
    )
```

profile of v0, /device:TPU:1, one launch (start us, length us, event | category | flops | bytes accessed | tf_op | source)
XLA Modules:
  0.0 262.0 jit_solution(7299178861073785476)
XLA Ops:
  0.7 1.3 reduce.3
  2.0 1.3 reshape_reshape_squeeze.3
  5.5 31.3 %while.24 = (s32[]{:T(128)}, f32[8,4,64,256]{3,2,0,1:T(8,128)}, f32[8,9,64,8]{2,3,1,0:T(8,128)S(1)}, s32[8,64,8]{2,1,0:T(8,128)S(1)}, s32[8,64]{1,0:T(8,128)S(1)...) while((s32[]{:T(128)}, f32[8,4,64,256]{3,2,0,1:T(8,128)}, ...), condition=%wide.region_3.4_spmd, body=%wide.region_0.3_spmd.sunk | while | flops 19023496 | bytes 2094577 | solution.py:112
  6.1 1.2 fusion.175
  10.0 1.2 fusion.175
  14.0 1.2 fusion.175
  17.9 1.2 fusion.175
  21.8 1.2 fusion.175
  25.7 1.2 fusion.175
  29.6 1.2 fusion.175
  33.5 1.2 fusion.175
  36.8 4.5 %copy.278 = f32[1,4,512,256]{3,1,0,2:T(4,128)} copy(f32[1,4,512,256]{3,2,1,0:T(8,128)} %bitcast.434) | data formatting | bytes 4194304 | tf_op jit(solution)/shard_map/broadcast_in_dim;reshape | solution.py:116
  41.3 11.5 %all-to-all-start = ((f32[1,4,512,256]{3,1,0,2:T(4,128)}), f32[1,4,512,256]{3,1,0,2:T(4,128)S(1)}, u32[]{:S(2)}, u32[]{:S(2)}) async-start(f32[1,4,512,256]{3,1,0,2:T(4,128)} %copy.278), calls=%async_computation | async-start | bytes 4194304 | tf_op jit(solution)/shard_map/all_to_all | solution.py:116
  54.7 1.1 fusion.94
  57.8 25.6 %all-to-all-done = f32[1,4,512,256]{3,1,0,2:T(4,128)S(1)} async-done(((f32[1,4,512,256]{3,1,0,2:T(4,128)}), f32[1,4,512,256]{3,1,0,2:T(4,128)S(1)}, u32[]{:S(2)}, u32[]{:S(2)}) %all-to-all-start) | async-done | bytes 2097184 | tf_op jit(solution)/shard_map/all_to_all | solution.py:116
  90.9 1.3 broadcast_in_dim.246
  108.1 1.8 copy.309
  109.9 4.5 %all-to-all-start.1 = ((f32[128,4,4,256]{3,2,1,0:T(4,128)}), f32[128,4,4,256]{3,2,1,0:T(4,128)S(1)}, u32[]{:S(2)}, u32[]{:S(2)}) async-start(f32[128,4,4,256]{3,2,1,0:T(4,128)} %bitcast.426), calls=%async_computation.1 | async-start | bytes 4194304 | tf_op jit(solution)/shard_map/all_to_all | solution.py:121
  115.0 30.0 %all-to-all-done.1 = f32[128,4,4,256]{3,2,1,0:T(4,128)S(1)} async-done(((f32[128,4,4,256]{3,2,1,0:T(4,128)}), f32[128,4,4,256]{3,2,1,0:T(4,128)S(1)}, u32[]{:S(2)}, u32[]{:S(2)}) %all-to-all-start.1) | async-done | bytes 2097184 | tf_op jit(solution)/shard_map/all_to_all | solution.py:121
  145.0 1.9 copy.310
  146.9 112.5 %while.25 = (s32[]{:T(128)}, f32[8,9,64,8]{2,3,1,0:T(8,128)S(1)}, f32[8,4,64,256]{3,1,2,0:T(4,128)}, s32[8,64,8]{2,1,0:T(8,128)}, f32[8,9,64,8]{2,3,1,0:T(8,128)...) while((s32[]{:T(128)}, f32[8,9,64,8]{2,3,1,0:T(8,128)S(1)}, ...), condition=%wide.region_24.25_spmd, body=%wide.region_13.24_spmd.sunk | while | flops 40832136 | bytes 7030313 | solution.py:136
  150.4 2.1 log-plus-one_reduce_fusion.2
  154.9 1.0 constant_dynamic-slice_fusion.8
  156.0 1.3 multiply_divide_fusion.3
  157.4 1.5 fusion.181
  164.4 2.1 log-plus-one_reduce_fusion.2
  169.0 1.0 constant_dynamic-slice_fusion.8
  170.0 1.3 multiply_divide_fusion.3
  171.4 1.5 fusion.181
  178.5 2.1 log-plus-one_reduce_fusion.2
  184.1 1.3 multiply_divide_fusion.3
  185.5 1.5 fusion.181
  192.5 2.1 log-plus-one_reduce_fusion.2
  198.1 1.3 multiply_divide_fusion.3
  199.5 1.5 fusion.181
  206.6 2.1 log-plus-one_reduce_fusion.2
  212.2 1.3 multiply_divide_fusion.3
  213.6 1.5 fusion.181
  220.7 2.1 log-plus-one_reduce_fusion.2
  226.3 1.3 multiply_divide_fusion.3
  227.7 1.5 fusion.181
  234.7 2.1 log-plus-one_reduce_fusion.2
  240.3 1.3 multiply_divide_fusion.3
  241.8 1.5 fusion.181
  248.8 2.1 log-plus-one_reduce_fusion.2
  254.4 1.3 multiply_divide_fusion.3
  255.8 1.5 fusion.181
  260.1 1.9 reshape.1612
  (596 shorter events, 121.3 us)
Async XLA Ops:
  0.6 54.0 %copy-start = (bf16[1024,384]{1,0:T(8,128)(2,1)S(1)}, bf16[1024,384]{1,0:T(8,128)(2,1)}, u32[]{:S(2)}) copy-start(bf16[1024,384]{1,0:T(8,128)(2,1)} %param.17) | copy-start | bytes 2359300
  3.3 0.7 copy-start.34
  3.4 1.4 copy-start.44
  36.8 4.5 %copy-start.6 = (f32[8,9,64,8]{2,3,1,0:T(8,128)}, f32[8,9,64,8]{2,3,1,0:T(8,128)S(1)}, u32[]{:S(2)}) copy-start(f32[8,9,64,8]{2,3,1,0:T(8,128)S(1)} %get-tuple-element.592) | copy-start | bytes 442372
  36.8 4.5 %copy-start.7 = (s32[8,64,8]{2,1,0:T(8,128)}, s32[8,64,8]{2,1,0:T(8,128)S(1)}, u32[]{:S(2)}) copy-start(s32[8,64,8]{2,1,0:T(8,128)S(1)} %get-tuple-element.593) | copy-start | bytes 49156
  36.8 4.5 %copy-start.38 = (s32[8,64]{1,0:T(8,128)}, s32[8,64]{1,0:T(8,128)S(1)}, u32[]{:S(2)}) copy-start(s32[8,64]{1,0:T(8,128)S(1)} %get-tuple-element.594) | copy-start | bytes 6148
  41.3 13.4 %copy-start.45 = (bf16[384]{0:T(512)(128)(2,1)S(1)}, bf16[384]{0:T(512)(128)(2,1)}, u32[]{:S(2)}) copy-start(bf16[384]{0:T(512)(128)(2,1)} %param.20) | copy-start | bytes 2308
  41.3 13.4 %copy-start.46 = (bf16[384,384]{1,0:T(8,128)(2,1)S(1)}, bf16[384,384]{1,0:T(8,128)(2,1)}, u32[]{:S(2)}) copy-start(bf16[384,384]{1,0:T(8,128)(2,1)} %param.18) | copy-start | bytes 884740
  41.3 13.4 %copy-start.47 = (f32[384]{0:T(512)S(1)}, f32[384]{0:T(512)}, u32[]{:S(2)}) copy-start(f32[384]{0:T(512)} %param.19) | copy-start | bytes 4612
  41.3 42.0 %all-to-all-start = ((f32[1,4,512,256]{3,1,0,2:T(4,128)}), f32[1,4,512,256]{3,1,0,2:T(4,128)S(1)}, u32[]{:S(2)}, u32[]{:S(2)}) async-start(f32[1,4,512,256]{3,1,0,2:T(4,128)} %copy.278), calls=%async_computation | async-start | bytes 4194304 | tf_op jit(solution)/shard_map/all_to_all | solution.py:116
  53.7 30.4 %copy-start.22 = (pred[64,4]{1,0:T(8,128)(4,1)}, pred[64,4]{1,0:T(8,128)(4,1)S(1)}, u32[]{:S(2)}) copy-start(pred[64,4]{1,0:T(8,128)(4,1)S(1)} %copy.274) | copy-start | bytes 772
  53.9 31.6 %copy-start.28 = (pred[32,4]{1,0:T(8,128)(4,1)}, pred[32,4]{1,0:T(8,128)(4,1)S(1)}, u32[]{:S(2)}) copy-start(pred[32,4]{1,0:T(8,128)(4,1)S(1)} %copy.273) | copy-start | bytes 388
  54.1 32.0 %copy-start.32 = (pred[16,4]{1,0:T(8,128)(4,1)}, pred[16,4]{1,0:T(8,128)(4,1)S(1)}, u32[]{:S(2)}) copy-start(pred[16,4]{1,0:T(8,128)(4,1)S(1)} %copy.272) | copy-start | bytes 196
  54.3 33.0 %copy-start.40 = (pred[8,4]{1,0:T(8,128)(4,1)}, pred[8,4]{1,0:T(8,128)(4,1)S(1)}, u32[]{:S(2)}) copy-start(pred[8,4]{1,0:T(8,128)(4,1)S(1)} %copy.271) | copy-start | bytes 100
  54.5 33.6 %copy-start.42 = (pred[4,4]{1,0:T(4,128)(4,1)}, pred[4,4]{1,0:T(4,128)(4,1)S(1)}, u32[]{:S(2)}) copy-start(pred[4,4]{1,0:T(4,128)(4,1)S(1)} %copy.270) | copy-start | bytes 52
  54.6 34.2 %copy-start.43 = (pred[2,4]{1,0:T(4,128)(4,1)}, pred[2,4]{1,0:T(4,128)(4,1)S(1)}, u32[]{:S(2)}) copy-start(pred[2,4]{1,0:T(4,128)(4,1)S(1)} %copy.269) | copy-start | bytes 28
  54.7 1.8 copy-start.25
  55.8 28.1 %copy-start.36 = (f32[1,1024]{1,0:T(1,128)}, f32[1,1024]{1,0:T(1,128)S(1)}, u32[]{:S(2)}) copy-start(f32[1,1024]{1,0:T(1,128)S(1)} %fusion.94) | copy-start | bytes 12292
  55.8 28.1 %copy-start.30 = (f32[1024]{0:T(1024)}, f32[1024]{0:T(1024)S(1)}, u32[]{:S(2)}) copy-start(f32[1024]{0:T(1024)S(1)} %multiply_divide_fusion.1) | copy-start | bytes 12292
  84.7 0.7 copy-start.2
  85.7 0.8 copy-start.1
  86.5 1.7 copy-start.4
  86.5 1.7 copy-start.8
  86.6 0.7 copy-start.12
  86.6 3.0 %copy-start.39 = (pred[4]{0:T(512)(128)(4,1)S(1)}, pred[4]{0:T(512)(128)(4,1)}, u32[]{:S(2)}) copy-start(pred[4]{0:T(512)(128)(4,1)} %fusion.138) | copy-start | bytes 16
  86.7 3.6 %copy-start.26 = (f32[3,1024]{1,0:T(4,128)S(1)}, f32[3,1024]{1,0:T(4,128)}, u32[]{:S(2)}) copy-start(f32[3,1024]{1,0:T(4,128)} %param.21) | copy-start | bytes 36868
  86.7 3.6 %copy-start.31 = (f32[1024]{0:T(1024)S(1)}, f32[1024]{0:T(1024)}, u32[]{:S(2)}) copy-start(f32[1024]{0:T(1024)} %copy-done.30) | copy-start | bytes 12292
  87.4 0.9 copy-start.9
  87.4 0.9 copy-start.11
  87.4 0.6 copy-start.16
  88.2 0.7 copy-start.14
  88.2 0.7 copy-start.15
  88.2 0.6 copy-start.20
  88.9 0.6 copy-start.19
  88.9 1.3 copy-start.24
  90.2 0.7 copy-start.27
  92.2 8.4 %copy-start.10 = (f32[8,4,4,256]{3,2,1,0:T(4,128)S(1)}, f32[8,4,4,256]{3,2,1,0:T(4,128)}, u32[]{:S(2)}) copy-start(f32[8,4,4,256]{3,2,1,0:T(4,128)} %copy-done.9) | copy-start | bytes 393220
  92.2 8.4 %copy-start.17 = (f32[8,4,256]{2,1,0:T(4,128)S(1)}, f32[8,4,256]{2,1,0:T(4,128)}, u32[]{:S(2)}) copy-start(f32[8,4,256]{2,1,0:T(4,128)} %copy-done.16) | copy-start | bytes 98308
  92.2 9.3 %copy-start.41 = (pred[8,4]{1,0:T(8,128)(4,1)S(1)}, pred[8,4]{1,0:T(8,128)(4,1)}, u32[]{:S(2)}) copy-start(pred[8,4]{1,0:T(8,128)(4,1)} %copy-done.40) | copy-start | bytes 100
  99.0 2.7 %copy-start.5 = (f32[16,4,4,256]{3,2,1,0:T(4,128)S(1)}, f32[16,4,4,256]{3,2,1,0:T(4,128)}, u32[]{:S(2)}) copy-start(f32[16,4,4,256]{3,2,1,0:T(4,128)} %copy-done.4) | copy-start | bytes 786436
  99.0 2.7 %copy-start.13 = (f32[16,4,256]{2,1,0:T(4,128)S(1)}, f32[16,4,256]{2,1,0:T(4,128)}, u32[]{:S(2)}) copy-start(f32[16,4,256]{2,1,0:T(4,128)} %copy-done.12) | copy-start | bytes 196612
  100.7 2.0 copy-start.33
  103.1 1.2 copy-start.29
  104.9 1.0 copy-start.3
  106.4 0.7 copy-start.23
  109.9 4.5 %copy-start.35 = (f32[1024]{0:T(1024)S(1)}, f32[1024]{0:T(1024)}, u32[]{:S(2)}) copy-start(f32[1024]{0:T(1024)} %get-tuple-element.231) | copy-start | bytes 12292
  109.9 4.5 %copy-start.37 = (f32[1,1024]{1,0:T(1,128)S(1)}, f32[1,1024]{1,0:T(1,128)}, u32[]{:S(2)}) copy-start(f32[1,1024]{1,0:T(1,128)} %copy-done.36) | copy-start | bytes 12292
  109.9 35.1 %all-to-all-start.1 = ((f32[128,4,4,256]{3,2,1,0:T(4,128)}), f32[128,4,4,256]{3,2,1,0:T(4,128)S(1)}, u32[]{:S(2)}, u32[]{:S(2)}) async-start(f32[128,4,4,256]{3,2,1,0:T(4,128)} %bitcast.426), calls=%async_computation.1 | async-start | bytes 4194304 | tf_op jit(solution)/shard_map/all_to_all | solution.py:121
  (2 other events, 1.2 us)
where the time goes:
time: 266 us; the launch traced here: 262 us
  other arithmetic  89.4 us (34%)
  local copies, waits for them, and re-layouts  60.1 us (23%)
  waiting for transfers between devices  55.6 us (21%)
  matrix products  38.1 us (14%)
  starting transfers between devices  16 us (6%)
    dot_general x24, matrix products, render_tiles(): jnp.einsum('tgh,thp->tgp', prior, log_trans, precision=lax.Precision.HIGH...  36.9 us
    all_to_all x1, waiting for transfers between devices, shards(): lax.all_to_all(adjoint, 'region', split_axis=0, concat_axis=2, tiled=True)  30 us
    all_to_all x1, waiting for transfers between devices, shards(): lax.all_to_all(partial_value[None], 'region', split_axis=2, concat_axis=0...  25.6 us
    split x16, local copies, waits for them, and re-layouts, render_tiles(): return jnp.concatenate([color_sum, transmit[None]], 0)  15.9 us
    reduce_sum x8, other arithmetic, render_tiles(): unit_y = delta_y * jnp.exp(-params[3])[:, :, None]  12.3 us
    all_to_all x1, starting transfers between devices, shards(): lax.all_to_all(partial_value[None], 'region', split_axis=2, concat_axis=0...  11.5 us
    reduce_sum x16, other arithmetic, render_tiles(): color_sum = jnp.sum(colors[:, :, :, None] * weight[None], 2)  8.84 us
    concatenate x14, other arithmetic, adjoint_pair(): jnp.concatenate([front_layer[:, 3:4] * grad_color, grad_trans * front_lay...  8.34 us
  transfers between devices with their start and end apart: 2, of which 2 were waited for; matrix products, arithmetic and copies ran while one was open for 2% of the time, Pallas kernels for 0%

commit v1 on v0

v1 whole, which is shorter than its diff:
```python
import math

import jax
import jax.numpy as jnp
import numpy as np
from jax import lax
from jax.experimental import pallas as pl
from jax.experimental.pallas import tpu as pltpu
from jax.sharding import PartitionSpec as P

TSIDE = 16
PIX = TSIDE * TSIDE
SPLATS = 8
LANES = 128
WIDTH = 384
HALF_LOG2E = 0.5 * math.log2(math.e)
F32 = jnp.float32
BF16 = jnp.bfloat16


def cut_columns(source, shift):
    return pltpu.roll(source, shift, 1) if shift else source


def pack_kernel(gauss_ref, depth_ref, cover_ref, out_ref, turned, strided):
    group = lax.broadcasted_iota(jnp.int32, (32, LANES), 1) // 32
    for part in range(3):
        for d in range(4):
            block = None
            for a in range(min(4, 9 - 4 * part)):
                moved = cut_columns(gauss_ref[4 * part + a], 32 * ((a - d) % 4))
                block = moved if block is None else jnp.where(group == a, moved, block)
            strided[part, pl.ds(d, 32, stride=4), :] = block
    ranks = depth_ref[...].astype(F32)
    covered = cover_ref[...].astype(F32)
    filler = jnp.zeros((LANES - 16, 512), F32)
    row = lax.broadcasted_iota(jnp.int32, (8, 512), 0)
    covered = jnp.where(row == 0, jnp.broadcast_to(covered, (8, 512)), 0.0)
    stacked = jnp.concatenate([ranks, covered, filler], 0)
    for b in range(4):
        turned[pl.ds(b * LANES, LANES), :] = stacked[:, b * LANES : (b + 1) * LANES].T
    tail = None
    for t in range(4):
        moved = pltpu.roll(turned[pl.ds(t, LANES, stride=4), :], 32 + 16 * t, 1)
        tail = moved if tail is None else tail + moved
    lane = lax.broadcasted_iota(jnp.int32, (LANES, LANES), 1)
    out_ref[:, 0:128] = strided[0]
    out_ref[:, 128:256] = strided[1]
    out_ref[:, 256:384] = jnp.where(lane < 32, strided[2], tail)


def unpack_kernel(msg_ref, out_ref, strided):
    group = lax.broadcasted_iota(jnp.int32, (32, LANES), 1) // 32
    for part in range(3):
        strided[part] = msg_ref[:, part * LANES : (part + 1) * LANES]
    for p in range(9):
        a, part = p % 4, p // 4
        block = None
        for d in range(4):
            moved = cut_columns(strided[part, pl.ds(d, 32, stride=4), :], 32 * ((d - a) % 4))
            block = moved if block is None else jnp.where(group == d, moved, block)
        out_ref[p] = block


def pixel_kernel(feat_ref, w_first_ref, b_first_ref, w_second_ref, target_ref, pix_ref):
    pre = jnp.dot(feat_ref[...], w_first_ref[...], preferred_element_type=F32) + b_first_ref[...]
    hidden = jax.nn.gelu(pre).astype(BF16)
    rows = jnp.broadcast_to(w_second_ref[...], (LANES, w_second_ref.shape[1]))
    score = lax.dot_general(hidden, rows, (((1,), (1,)), ((), ())), preferred_element_type=F32)
    spread = 0.5 + (jnp.maximum(score, 0.0) + jnp.log1p(jnp.exp(-jnp.abs(score))))
    filler = jnp.zeros((LANES - 3, PIX), F32)
    wanted = jnp.concatenate([target_ref[...], filler], 0).T
    lane = lax.broadcasted_iota(jnp.int32, (PIX, LANES), 1)
    pix_ref[...] = jnp.where(
        lane == 3, 1.0 / (spread * spread), jnp.where(lane == 4, jnp.log(spread), wanted)
    )


def split_dot(value, matrix):
    high = value.astype(BF16)
    low = (value - high.astype(F32)).astype(BF16)
    return jnp.dot(high, matrix, preferred_element_type=F32) + jnp.dot(
        low, matrix, preferred_element_type=F32
    )


ROWS = 4
STEPS = TSIDE // ROWS


def splat_kernel(
    msg_ref, pix_ref, before_ref, behind_ref, loss_ref, out_ref,
    turned, rows, across, alphas, weights, clear, color, carry, sums, grads,
):
    for b in range(3):
        turned[pl.ds(b * LANES, LANES), :] = msg_ref[:, b * LANES : (b + 1) * LANES].T
    sub = lax.broadcasted_iota(jnp.int32, (8, LANES), 0).astype(F32)
    eye = lax.broadcasted_iota(jnp.int32, (LANES, LANES), 0) == lax.broadcasted_iota(
        jnp.int32, (LANES, LANES), 1
    )

    def tile(t, unused):
        def raw(p):
            return turned[pl.ds(pl.multiple_of(32 * p + 8 * t, 8), 8), :]

        ranks = turned[pl.ds(pl.multiple_of(288 + 16 * t, 8), 8), :]
        covered = turned[pl.ds(288 + 16 * t + 8, 1), :]
        inv_x = jnp.exp(-raw(2))
        inv_y = jnp.exp(-raw(3))
        curl = jnp.tanh(raw(4))
        rho = 0.9 * curl
        inv_det = 1.0 / (1.0 - rho * rho)
        scale = jnp.sqrt(HALF_LOG2E * inv_det)
        odds = jax.nn.sigmoid(raw(5))
        tint = [jax.nn.sigmoid(raw(6 + c)) for c in range(3)]
        plain = [raw(0), raw(1), inv_x * scale, inv_y * scale, 2.0 * rho, 0.99 * odds * covered] + tint

        for k in range(SPLATS):
            chosen = ranks == float(k)
            for n, value in enumerate(plain):
                row = jnp.sum(jnp.where(chosen, value, 0.0), axis=0, keepdims=True)
                rows[k * 9 + n] = jnp.broadcast_to(row, (8, LANES))
            for h in range(2):
                unit = (sub + (0.5 + 8.0 * h) - rows[k * 9]) * rows[k * 9 + 2]
                across[k, h, 0] = unit
                across[k, h, 1] = unit * rows[k * 9 + 4]
                across[k, h, 2] = unit * unit

        def unit_y(k, r, step):
            at = (step * ROWS + r).astype(F32) + 0.5
            return (at - rows[k * 9 + 1]) * rows[k * 9 + 3]

        def render(step, unused):
            trans = [[None] * 2 for _ in range(ROWS)]
            total = [[[None] * 3 for _ in range(2)] for _ in range(ROWS)]
            for k in range(SPLATS):
                opacity = rows[k * 9 + 5]
                shade = [rows[k * 9 + 6 + c] for c in range(3)]
                for r in range(ROWS):
                    down = unit_y(k, r, step)
                    for h in range(2):
                        power = down * (across[k, h, 1] - down) - across[k, h, 2]
                        alpha = opacity * jnp.exp2(power)
                        weight = alpha if k == 0 else trans[r][h] * alpha
                        trans[r][h] = 1.0 - alpha if k == 0 else trans[r][h] - weight
                        alphas[step, k, 2 * r + h] = alpha
                        weights[step, k, 2 * r + h] = weight
                        for c in range(3):
                            term = weight * shade[c]
                            total[r][h][c] = term if k == 0 else total[r][h][c] + term
            for r in range(ROWS):
                for h in range(2):
                    at = pl.ds(pl.multiple_of((step * ROWS + r) * 16 + 8 * h, 8), 8)
                    clear[at, :] = trans[r][h]
                    for c in range(3):
                        color[c, at, :] = total[r][h][c]
            return 0

        lax.fori_loop(0, STEPS, render, 0)

        through = clear[...]
        logs = split_dot(jnp.log(through), before_ref[t])
        ahead = jnp.exp(logs[:, :LANES])
        whole = jnp.exp(logs[:, LANES:])
        pix = pix_ref[pl.ds(pl.multiple_of(t * PIX, PIX), PIX), :]
        inv_square = jnp.broadcast_to(pix[:, 3:4], (PIX, LANES))
        ones = jnp.ones((LANES, LANES), BF16)
        squares = None
        grad_trans = None
        along = None
        for c in range(3):
            layer = ahead * color[c]
            residual = split_dot(layer, ones) + whole - pix[:, c : c + 1]
            slope = residual * inv_square
            squares = residual * residual if c == 0 else squares + residual * residual
            grad_trans = slope if c == 0 else grad_trans + slope
            along = slope * layer if c == 0 else along + slope * layer
            color[c] = ahead * slope
        loss = 0.5 * squares * inv_square + pix[:, 4:5]
        for h in range(2):
            line = jnp.where(eye, loss[h * LANES : (h + 1) * LANES], 0.0)
            loss_ref[pl.ds(2 * t + h, 1), :] = jnp.sum(line, axis=0, keepdims=True)
        follow = split_dot(along, behind_ref[t]) + grad_trans * whole
        carry[...] = follow / through

        sums[...] = jnp.zeros_like(sums)

        def pull(step, unused):
            behind = [None] * (2 * ROWS)
            slope = [[None] * 3 for _ in range(2 * ROWS)]
            for n in range(2 * ROWS):
                at = pl.ds(pl.multiple_of(step * (ROWS * 16) + 8 * n, 8), 8)
                behind[n] = carry[at, :]
                slope[n] = [color[c, at, :] for c in range(3)]
            for k in range(SPLATS - 1, -1, -1):
                shade = [rows[k * 9 + 6 + c] for c in range(3)]
                acc = [None] * 9

                def add(n, value):
                    acc[n] = value if acc[n] is None else acc[n] + value

                for r in range(ROWS):
                    down = unit_y(k, r, step)
                    for h in range(2):
                        n = 2 * r + h
                        alpha = alphas[step, k, n]
                        weight = weights[step, k, n]
                        gain = slope[n][0] * shade[0] + slope[n][1] * shade[1] + slope[n][2] * shade[2]
                        change = gain - behind[n]
                        behind[n] = behind[n] + alpha * change
                        pulled = weight * change
                        leaned = pulled * down
                        add(3 * h, pulled)
                        add(3 * h + 1, leaned)
                        add(3 * h + 2, leaned * down)
                        for c in range(3):
                            add(6 + c, weight * slope[n][c])
                for n in range(9):
                    sums[k * 9 + n] = sums[k * 9 + n] + acc[n]
            return 0

        lax.fori_loop(0, STEPS, pull, 0)

        plain_sums = [None] * 9
        for k in range(SPLATS):
            chosen = ranks == float(k)
            left, right = [[sums[k * 9 + 3 * h + n] for n in range(3)] for h in range(2)]
            u0, u1 = across[k, 0, 0], across[k, 1, 0]
            m0, m1 = left[0] * u0, right[0] * u1
            moments = [
                left[0] + right[0],
                m0 + m1,
                left[1] + right[1],
                m0 * u0 + m1 * u1,
                left[1] * u0 + right[1] * u1,
                left[2] + right[2],
            ] + [sums[k * 9 + 6 + c] for c in range(3)]
            for n, value in enumerate(moments):
                line = jnp.broadcast_to(jnp.sum(value, axis=0, keepdims=True), (8, LANES))
                plain_sums[n] = (
                    jnp.where(chosen, line, 0.0) if k == 0 else jnp.where(chosen, line, plain_sums[n])
                )
        s0, su, sv, suu, suv, svv = plain_sums[:6]
        inv_scale = 1.0 / scale
        su, sv = su * inv_scale, sv * inv_scale
        inv_both = inv_scale * inv_scale
        suu, suv, svv = suu * inv_both, suv * inv_both, svv * inv_both
        result = [
            inv_det * inv_x * (su - rho * sv),
            inv_det * inv_y * (sv - rho * su),
            inv_det * (suu - rho * suv),
            inv_det * (svv - rho * suv),
            inv_det
            * (suv - rho * inv_det * (suu - 2.0 * rho * suv + svv))
            * (0.9 * (1.0 - curl * curl)),
            s0 * (1.0 - odds),
        ] + [plain_sums[6 + c] * tint[c] * (1.0 - tint[c]) for c in range(3)]
        for p in range(9):
            grads[pl.ds(pl.multiple_of(32 * p + 8 * t, 8), 8), :] = result[p]
        return 0

    grads[pl.ds(288, 96), :] = jnp.zeros((96, LANES), F32)
    lax.fori_loop(0, 4, tile, 0)
    for b in range(3):
        out_ref[:, b * LANES : (b + 1) * LANES] = grads[pl.ds(b * LANES, LANES), :].T


def order_matrix(regions):
    levels = regions.bit_length() - 1
    turns = np.zeros((regions - 1, regions), np.float32)
    for r in range(regions):
        for d in range(levels):
            bit = (r >> (levels - 1 - d)) & 1
            turns[2**d - 1 + (r >> (levels - d)), r] = (1 - 2 * bit) * 2 ** (levels - 1 - d)
    return turns


def vmem(*shape, dtype=F32):
    return pltpu.VMEM(shape, dtype)


def shards(gaussians, depth, coverage, flips, features, w_first, b_first, w_second, target):
    regions = lax.axis_size("region")
    my_index = lax.axis_index("region")
    limit = pltpu.CompilerParams(vmem_limit_bytes=32 * 1024 * 1024)

    message = pl.pallas_call(
        pack_kernel,
        out_shape=jax.ShapeDtypeStruct((regions, WIDTH), F32),
        scratch_shapes=[vmem(512, LANES), vmem(3, LANES, LANES)],
        compiler_params=limit,
        name="pack",
    )(gaussians.reshape(9, 32, LANES), depth[0].T, coverage)
    received = lax.all_to_all(message, "region", 0, 0, tiled=True)

    pix = pl.pallas_call(
        pixel_kernel,
        grid=(4,),
        in_specs=[
            pl.BlockSpec((PIX, 384), lambda i: (i, 0)),
            pl.BlockSpec((384, 384), lambda i: (0, 0)),
            pl.BlockSpec((1, 384), lambda i: (0, 0)),
            pl.BlockSpec((1, 384), lambda i: (0, 0)),
            pl.BlockSpec((3, PIX), lambda i: (0, i)),
        ],
        out_specs=pl.BlockSpec((PIX, LANES), lambda i: (i, 0)),
        out_shape=jax.ShapeDtypeStruct((4 * PIX, LANES), F32),
        compiler_params=limit,
        cost_estimate=pl.CostEstimate(
            flops=2 * 1024 * 384 * 512, bytes_accessed=2_000_000, transcendentals=1024 * 384
        ),
        name="pixels",
    )(features, w_first, b_first[None], w_second[None], target)

    my_flips = lax.dynamic_slice_in_dim(flips, my_index * 4, 4, 0).astype(F32)
    turned = jnp.dot(my_flips, jnp.asarray(order_matrix(regions)), precision=lax.Precision.HIGHEST)
    rank = jnp.arange(regions, dtype=F32)[None] + turned
    before = (rank[:, :, None] < rank[:, None, :]).astype(BF16)
    behind = (rank[:, :, None] > rank[:, None, :]).astype(BF16)
    before = jnp.concatenate([before, jnp.ones_like(before)], 2)

    loss, returned = pl.pallas_call(
        splat_kernel,
        out_shape=(
            jax.ShapeDtypeStruct((8, LANES), F32),
            jax.ShapeDtypeStruct((regions, WIDTH), F32),
        ),
        scratch_shapes=[
            vmem(WIDTH, LANES),
            vmem(72, 8, LANES),
            vmem(SPLATS, 2, 3, 8, LANES),
            vmem(STEPS, SPLATS, 2 * ROWS, 8, LANES),
            vmem(STEPS, SPLATS, 2 * ROWS, 8, LANES),
            vmem(PIX, LANES),
            vmem(3, PIX, LANES),
            vmem(PIX, LANES),
            vmem(72, 8, LANES),
            vmem(WIDTH, LANES),
        ],
        compiler_params=limit,
        name="splats",
    )(received, pix, before, behind)

    back = lax.all_to_all(returned, "region", 0, 0, tiled=True)
    splat_grads = pl.pallas_call(
        unpack_kernel,
        out_shape=jax.ShapeDtypeStruct((9, 32, LANES), F32),
        scratch_shapes=[vmem(3, LANES, LANES)],
        compiler_params=limit,
        name="unpack",
    )(back)
    return loss.reshape(4 * PIX), splat_grads.reshape(1, 9, 32 * LANES)


def solution(mesh):
    placed = (
        P("region", None, None),
        P("region", None, None),
        P("region", None),
        P(),
        P("region", None),
        P(),
        P(),
        P(),
        P(None, "region"),
    )
    return jax.shard_map(
        shards,
        mesh=mesh,
        in_specs=placed,
        out_specs=(P("region"), P("region", None, None)),
        check_vma=False,
    )
```

time: 266 us -> 51.6 us (0.19); the launches traced: 262 us -> 51.3 us
  other arithmetic: 89.4 us -> 0.18 us
  local copies, waits for them, and re-layouts: 60.1 us -> 4.72 us
  waiting for transfers between devices: 55.6 us -> 6.13 us
  matrix products: 38.1 us -> 0.84 us
  blocking collectives: 0 us -> 14.5 us
  Pallas kernels: 0 us -> 12.6 us
  starting transfers between devices: 16 us -> 11.5 us
    all_to_all x2 -> x1, waiting for transfers between devices: 55.6 us -> 6.13 us  [shards(): received = lax.all_to_all(message, 'region', 0, 0, tiled=True)]
    dot_general x25 -> x1, matrix products: 38.1 us -> 0.84 us  [shards(): jnp.dot(my_flips, jnp.asarray(order_matrix(regions)), precision=lax.Preci...]
    reduce_sum x33 -> x0, other arithmetic: 26.9 us -> none  [the longest x8 12.3 us: render_tiles(): unit_y = delta_y * jnp.exp(-params[3])[:, :, None]]
    mul x63 -> x0, other arithmetic: 24.4 us -> none  [the longest x8 6.1 us: render_tiles(): jax.nn.sigmoid(params[5])]
    split x16 -> x0, local copies, waits for them, and re-layouts: 15.9 us -> none  [render_tiles(): return jnp.concatenate([color_sum, transmit[None]], 0)]
    all_to_all x0 -> x1, blocking collectives: none -> 14.5 us  [shards(): back = lax.all_to_all(returned, 'region', 0, 0, tiled=True)]
    pallas_call x0 -> x4, Pallas kernels: none -> 12.6 us  [the longest x1 9.32 us: shards(): pl.pallas_call(splat_kernel, out_shape=(jax.ShapeDtypeStruct((8, LANES),...]
    concatenate x19 -> x1, other arithmetic: 8.84 us -> 0.04 us  [shards(): before = jnp.concatenate([before, jnp.ones_like(before)], 2)]
  transfers between devices with their start and end apart: 2 -> 1, of which waited for: 2 -> 1; matrix products, arithmetic and copies ran while one was open for 2% -> 2% of each run, Pallas kernels for 0% -> 4%
where the time goes in v1:
time: 51.6 us; the launch traced here: 51.3 us
  blocking collectives  14.5 us (28%)
  Pallas kernels  12.6 us (24%)
  starting transfers between devices  11.5 us (22%)
  waiting for transfers between devices  6.13 us (12%)
  local copies, waits for them, and re-layouts  4.72 us (9%)
  matrix products  0.84 us (2%)
  between operations  0.74 us (1%)
    all_to_all x1, blocking collectives, shards(): back = lax.all_to_all(returned, 'region', 0, 0, tiled=True)  14.5 us
    all_to_all x1, starting transfers between devices, shards(): received = lax.all_to_all(message, 'region', 0, 0, tiled=True)  11.5 us
    pallas_call x1, Pallas kernels, shards(): pl.pallas_call(splat_kernel, out_shape=(jax.ShapeDtypeStruct((8, LANES),...  9.32 us
    all_to_all x1, waiting for transfers between devices, shards(): received = lax.all_to_all(message, 'region', 0, 0, tiled=True)  6.13 us
    unnamed x20, local copies, waits for them, and re-layouts  3.63 us
    pallas_call x1, Pallas kernels, shards(): pl.pallas_call(pixel_kernel, grid=(4,), in_specs=[pl.BlockSpec((PIX, 384)...  2.1 us
  transfers between devices with their start and end apart: 1, of which 1 were waited for; matrix products, arithmetic and copies ran while one was open for 2% of the time, Pallas kernels for 4%

profile of v1, /device:TPU:1, one launch (start us, length us, event | category | flops | bytes accessed | tf_op | source)
XLA Modules:
  0.0 51.3 jit_solution(16833143235812156217)
XLA Ops:
  0.6 0.0 copy-start
  0.6 0.0 copy-start.2
  0.7 1.0 %copy-done.2 = f32[1,9,4096]{2,0,1:T(1,128)S(1)} copy-done((f32[1,9,4096]{2,0,1:T(1,128)S(1)}, f32[1,9,4096]{2,0,1:T(1,128)}, u32[]{:S(2)}) %copy-start.2) | copy-done | bytes 147480
  1.6 0.0 copy-start.4
  1.6 0.7 %copy-done.4 = s32[1,512,8]{1,2,0:T(8,128)S(1)} copy-done((s32[1,512,8]{1,2,0:T(8,128)S(1)}, s32[1,512,8]{1,2,0:T(8,128)}, u32[]{:S(2)}) %copy-start.4) | copy-done | bytes 16408
  2.3 0.0 copy-start.5
  2.3 0.7 %copy-done.5 = s32[1,512]{1,0:T(1,128)S(1)} copy-done((s32[1,512]{1,0:T(1,128)S(1)}, s32[1,512]{1,0:T(1,128)}, u32[]{:S(2)}) %copy-start.5) | copy-done | bytes 2072
  3.0 0.3 pack.1
  3.4 0.9 %copy.14 = f32[128,1,384]{2,1,0:T(1,128)} copy(f32[128,1,384]{2,0,1:T(8,128)S(1)} %bitcast.15) | data formatting | bytes 393216 | tf_op jit(solution)/shard_map/all_to_all | solution.py:294
  4.3 0.0 copy-start.6
  4.3 0.0 copy-start.1
  4.3 11.5 %all-to-all-start = ((f32[128,1,384]{2,1,0:T(1,128)}), f32[128,1,384]{2,1,0:T(1,128)S(1)}, u32[]{:S(2)}, u32[]{:S(2)}) async-start(f32[128,1,384]{2,1,0:T(1,128)} %copy.14), calls=%async_computation | async-start | bytes 393216 | tf_op jit(solution)/shard_map/all_to_all | solution.py:294
  15.8 0.0 copy-done.6
  15.8 0.8 %convolution_add_fusion = f32[4,128]{1,0:T(4,128)S(1)} fusion(f32[127,128]{1,0:T(8,128)S(1)} %copy-done.6, s32[512,127]{1,0:T(8,128)} %param.13, s32[]{:T(128)S(6)} %select_n.3), kind=kOutput, calls=%fused_computation | convolution fusion | flops 781308 | bytes 69124 | tf_op jit(solution)/shard_map/dot_general | solution.py:316
  16.6 0.0 copy-start.7
  16.6 0.0 copy-start.3
  16.6 0.1 compare_convert_fusion
  16.8 0.5 %copy-done.7 = f32[384]{0:T(512)S(1)} copy-done((f32[384]{0:T(512)S(1)}, f32[384]{0:T(512)}, u32[]{:S(2)}) %copy-start.7) | copy-done | bytes 1560
  17.3 0.0 copy-start.8
  17.3 0.7 %copy-done.8 = bf16[384]{0:T(512)(128)(2,1)S(1)} copy-done((bf16[384]{0:T(512)(128)(2,1)S(1)}, bf16[384]{0:T(512)(128)(2,1)}, u32[]{:S(2)}) %copy-start.8) | copy-done | bytes 792
  18.0 0.0 copy-done
  18.0 0.0 copy-done.1
  18.0 0.0 copy-done.3
  18.0 2.1 %pixels.1.pix_ref = f32[1024,128]{1,0:T(8,128)S(1)} custom-call(bf16[1024,384]{1,0:T(8,128)(2,1)S(1)} %copy-done, bf16[384,384]{1,0:T(8,128)(2,1)S(1)} %copy-done.1, f32[1,384]{1,0:T(1,128)S(1)} %broadcast_in_dim.4.b_first_ref, bf16[1,384]{1,0:T(2,128)(2,1)S(1)} %broadcast_in_dim.5.w_second_ref, f32[3,1024]{1,0:T(4,128)S(1)} %copy-done.3), custom_call_target="tpu_custom_call" | custom-call | flops 402653184 | bytes 2000000 | tf_op jit(solution)/shard_map/pixels/pallas_call | solution.py:296
  20.2 6.1 %all-to-all-done = f32[128,1,384]{2,1,0:T(1,128)S(1)} async-done(((f32[128,1,384]{2,1,0:T(1,128)}), f32[128,1,384]{2,1,0:T(1,128)S(1)}, u32[]{:S(2)}, u32[]{:S(2)}) %all-to-all-start) | async-done | bytes 196640 | tf_op jit(solution)/shard_map/all_to_all | solution.py:294
  26.3 9.3 %splats.1 = (f32[8,128]{1,0:T(8,128)}, f32[128,384]{1,0:T(8,128)S(1)}) custom-call(f32[128,384]{1,0:T(8,128)S(1)} %bitcast.17, f32[1024,128]{1,0:T(8,128)S(1)} %pixels.1.pix_ref, bf16[4,128,256]{2,1,0:T(8,128)(2,1)S(1)} %pad_convert_fusion.before_ref, bf16[4,128,128]{2,1,0:T(8,128)(2,1)S(1)} %get-tuple-element.12.behind_ref), custom_call_target="tpu_custom_call" | custom-call | tf_op jit(solution)/shard_map/splats/pallas_call | solution.py:322
  35.6 0.2 copy.15
  35.8 14.5 %all_to_all.22 = f32[128,1,384]{2,1,0:T(1,128)S(1)} all-to-all(f32[128,1,384]{2,1,0:T(1,128)S(1)} %copy.15), channel_id=1, replica_groups=mesh['region'=128] {'region'}, dimensions={0} | all-to-all | bytes 393216 | tf_op jit(solution)/shard_map/all_to_all | solution.py:344
  50.4 0.9 %unpack.1 = f32[9,32,128]{2,1,0:T(8,128)} custom-call(f32[128,384]{1,0:T(8,128)S(1)} %bitcast.16), custom_call_target="tpu_custom_call" | custom-call | tf_op jit(solution)/shard_map/unpack/pallas_call | solution.py:345
  (5 shorter events, 0.1 us)
Async XLA Ops:
  0.6 17.4 %copy-start = (bf16[1024,384]{1,0:T(8,128)(2,1)S(1)}, bf16[1024,384]{1,0:T(8,128)(2,1)}, u32[]{:S(2)}) copy-start(bf16[1024,384]{1,0:T(8,128)(2,1)} %feat_ref.1) | copy-start | bytes 2359300
  0.6 1.0 %copy-start.2 = (f32[1,9,4096]{2,0,1:T(1,128)S(1)}, f32[1,9,4096]{2,0,1:T(1,128)}, u32[]{:S(2)}) copy-start(f32[1,9,4096]{2,0,1:T(1,128)} %param.10) | copy-start | bytes 442372
  1.6 0.7 %copy-start.4 = (s32[1,512,8]{1,2,0:T(8,128)S(1)}, s32[1,512,8]{1,2,0:T(8,128)}, u32[]{:S(2)}) copy-start(s32[1,512,8]{1,2,0:T(8,128)} %param.11) | copy-start | bytes 49156
  2.3 0.7 %copy-start.5 = (s32[1,512]{1,0:T(1,128)S(1)}, s32[1,512]{1,0:T(1,128)}, u32[]{:S(2)}) copy-start(s32[1,512]{1,0:T(1,128)} %cover_ref.1) | copy-start | bytes 6148
  4.3 11.5 %copy-start.6 = (f32[127,128]{1,0:T(8,128)S(1)}, f32[127,128]{1,0:T(8,128)}, u32[]{:S(2)}) copy-start(f32[127,128]{1,0:T(8,128)} %constant.15.clone) | copy-start | bytes 195076
  4.3 13.8 %copy-start.1 = (bf16[384,384]{1,0:T(8,128)(2,1)S(1)}, bf16[384,384]{1,0:T(8,128)(2,1)}, u32[]{:S(2)}) copy-start(bf16[384,384]{1,0:T(8,128)(2,1)} %w_first_ref.1) | copy-start | bytes 884740
  4.3 22.0 %all-to-all-start = ((f32[128,1,384]{2,1,0:T(1,128)}), f32[128,1,384]{2,1,0:T(1,128)S(1)}, u32[]{:S(2)}, u32[]{:S(2)}) async-start(f32[128,1,384]{2,1,0:T(1,128)} %copy.14), calls=%async_computation | async-start | bytes 393216 | tf_op jit(solution)/shard_map/all_to_all | solution.py:294
  16.6 0.7 %copy-start.7 = (f32[384]{0:T(512)S(1)}, f32[384]{0:T(512)}, u32[]{:S(2)}) copy-start(f32[384]{0:T(512)} %param.16) | copy-start | bytes 4612
  16.6 1.4 %copy-start.3 = (f32[3,1024]{1,0:T(4,128)S(1)}, f32[3,1024]{1,0:T(4,128)}, u32[]{:S(2)}) copy-start(f32[3,1024]{1,0:T(4,128)} %target_ref.1) | copy-start | bytes 36868
  17.3 0.7 %copy-start.8 = (bf16[384]{0:T(512)(128)(2,1)S(1)}, bf16[384]{0:T(512)(128)(2,1)}, u32[]{:S(2)}) copy-start(bf16[384]{0:T(512)(128)(2,1)} %param.17) | copy-start | bytes 2308

commit v2 on v1

--- a/solution.py
+++ b/solution.py
@@ -30,7 +30,10 @@
             for a in range(min(4, 9 - 4 * part)):
                 moved = cut_columns(gauss_ref[4 * part + a], 32 * ((a - d) % 4))
                 block = moved if block is None else jnp.where(group == a, moved, block)
-            strided[part, pl.ds(d, 32, stride=4), :] = block
+            if part < 2:
+                out_ref[pl.ds(3 * d + part, 32, stride=12), :] = block
+            else:
+                strided[pl.ds(d, 32, stride=4), :] = block
     ranks = depth_ref[...].astype(F32)
     covered = cover_ref[...].astype(F32)
     filler = jnp.zeros((LANES - 16, 512), F32)
@@ -44,20 +47,16 @@
         moved = pltpu.roll(turned[pl.ds(t, LANES, stride=4), :], 32 + 16 * t, 1)
         tail = moved if tail is None else tail + moved
     lane = lax.broadcasted_iota(jnp.int32, (LANES, LANES), 1)
-    out_ref[:, 0:128] = strided[0]
-    out_ref[:, 128:256] = strided[1]
-    out_ref[:, 256:384] = jnp.where(lane < 32, strided[2], tail)
-
-
-def unpack_kernel(msg_ref, out_ref, strided):
+    out_ref[pl.ds(2, LANES, stride=3), :] = jnp.where(lane < 32, strided[...], tail)
+
+
+def unpack_kernel(msg_ref, out_ref):
     group = lax.broadcasted_iota(jnp.int32, (32, LANES), 1) // 32
-    for part in range(3):
-        strided[part] = msg_ref[:, part * LANES : (part + 1) * LANES]
     for p in range(9):
         a, part = p % 4, p // 4
         block = None
         for d in range(4):
-            moved = cut_columns(strided[part, pl.ds(d, 32, stride=4), :], 32 * ((d - a) % 4))
+            moved = cut_columns(msg_ref[pl.ds(3 * d + part, 32, stride=12), :], 32 * ((d - a) % 4))
             block = moved if block is None else jnp.where(group == d, moved, block)
         out_ref[p] = block
 
@@ -90,21 +89,62 @@
 
 def splat_kernel(
     msg_ref, pix_ref, before_ref, behind_ref, loss_ref, out_ref,
-    turned, rows, across, alphas, weights, clear, color, carry, sums, grads,
+    turned, places, sources, rows, across, alphas, weights, clear, color, carry, sums, grads,
 ):
     for b in range(3):
-        turned[pl.ds(b * LANES, LANES), :] = msg_ref[:, b * LANES : (b + 1) * LANES].T
+        turned[pl.ds(b * LANES, LANES), :] = msg_ref[pl.ds(b, LANES, stride=3), :].T
     sub = lax.broadcasted_iota(jnp.int32, (8, LANES), 0).astype(F32)
-    eye = lax.broadcasted_iota(jnp.int32, (LANES, LANES), 0) == lax.broadcasted_iota(
-        jnp.int32, (LANES, LANES), 1
-    )
-
-    def tile(t, unused):
+    lane = lax.broadcasted_iota(jnp.int32, (LANES, LANES), 1)
+    line = lax.broadcasted_iota(jnp.int32, (LANES, LANES), 0)
+
+    counts = []
+    for t in range(4):
+        kept = jnp.where(lane[:1] == 0, 1.0, turned[pl.ds(288 + 16 * t + 8, 1), :])
+        counts.append(jnp.sum(kept).astype(jnp.int32))
+        earlier = before_ref[t] if t % 2 == 0 else behind_ref[t]
+        spot = jnp.dot(
+            jnp.broadcast_to(kept, (8, LANES)).astype(BF16), earlier, preferred_element_type=F32
+        )
+        spot = spot if t % 2 == 0 else (LANES - 1.0) - spot
+        spot = jnp.where(kept > 0.0, spot, -1.0).astype(jnp.int32)
+        places[t] = spot
+        hit = jnp.broadcast_to(spot[:1].astype(F32), (LANES, LANES)).T == lane.astype(F32)
+        source = jnp.sum(jnp.where(hit, line.astype(F32), 0.0), axis=0, keepdims=True)
+        sources[t] = jnp.broadcast_to(source, (8, LANES)).astype(jnp.int32)
+
+    def block(i, unused):
+        pair, second = i // 2, i % 2
+        first_count = jnp.where(pair == 0, counts[0], counts[2])
+        last_count = jnp.where(pair == 0, counts[1], counts[3])
+        fits = first_count + last_count <= LANES
+        has_first = jnp.logical_or(fits, second == 0)
+        has_last = jnp.logical_or(fits, second == 1)
+        border = jnp.where(has_first, jnp.where(has_last, first_count, LANES), 0)
+
+        @pl.when(jnp.logical_not(jnp.logical_and(fits, second == 1)))
+        def _():
+            both_tiles(2 * pair, has_first, has_last, first_count, last_count, border)
+
+        return 0
+
+    def both_tiles(t, has_first, has_last, first_count, last_count, border):
+        flat = lane[:8]
+        in_first = flat < jnp.where(has_first, first_count, 0)
+        in_last = flat >= jnp.where(has_last, LANES - last_count, LANES)
+        first_source, last_source = sources[t], sources[t + 1]
+
+        def pick(at, step):
+            left = turned[pl.ds(pl.multiple_of(at, 8), 8), :]
+            right = turned[pl.ds(pl.multiple_of(at + step, 8), 8), :]
+            left = jnp.take_along_axis(left, first_source, axis=1)
+            right = jnp.take_along_axis(right, last_source, axis=1)
+            return jnp.where(in_first, left, jnp.where(in_last, right, 0.0))
+
         def raw(p):
-            return turned[pl.ds(pl.multiple_of(32 * p + 8 * t, 8), 8), :]
-
-        ranks = turned[pl.ds(pl.multiple_of(288 + 16 * t, 8), 8), :]
-        covered = turned[pl.ds(288 + 16 * t + 8, 1), :]
+            return pick(32 * p + 8 * t, 8)
+
+        ranks = pick(288 + 16 * t, 16)
+        covered = pick(288 + 16 * t + 8, 16)[:1]
         inv_x = jnp.exp(-raw(2))
         inv_y = jnp.exp(-raw(3))
         curl = jnp.tanh(raw(4))
@@ -159,28 +199,45 @@
         lax.fori_loop(0, STEPS, render, 0)
 
         through = clear[...]
-        logs = split_dot(jnp.log(through), before_ref[t])
+        same = (lane < border) == (line < border)
+        to_left = jnp.where(jnp.logical_and(same, line < lane), 1.0, 0.0).astype(BF16)
+        to_right = jnp.where(jnp.logical_and(same, line > lane), 1.0, 0.0).astype(BF16)
+        same = jnp.where(same, 1.0, 0.0).astype(BF16)
+        logs = split_dot(jnp.log(through), jnp.concatenate([to_left, same], 1))
         ahead = jnp.exp(logs[:, :LANES])
         whole = jnp.exp(logs[:, LANES:])
-        pix = pix_ref[pl.ds(pl.multiple_of(t * PIX, PIX), PIX), :]
-        inv_square = jnp.broadcast_to(pix[:, 3:4], (PIX, LANES))
-        ones = jnp.ones((LANES, LANES), BF16)
+        left_pix = pix_ref[pl.ds(pl.multiple_of(t * PIX, PIX), PIX), :]
+        right_pix = pix_ref[pl.ds(pl.multiple_of((t + 1) * PIX, PIX), PIX), :]
+        on_left = lax.broadcasted_iota(jnp.int32, (PIX, LANES), 1) < border
+
+        def field(n):
+            return jnp.where(on_left, left_pix[:, n : n + 1], right_pix[:, n : n + 1])
+
+        inv_square = field(3)
         squares = None
         grad_trans = None
         along = None
         for c in range(3):
             layer = ahead * color[c]
-            residual = split_dot(layer, ones) + whole - pix[:, c : c + 1]
+            residual = split_dot(layer, same) + whole - field(c)
             slope = residual * inv_square
             squares = residual * residual if c == 0 else squares + residual * residual
             grad_trans = slope if c == 0 else grad_trans + slope
             along = slope * layer if c == 0 else along + slope * layer
             color[c] = ahead * slope
-        loss = 0.5 * squares * inv_square + pix[:, 4:5]
+        loss = 0.5 * squares * inv_square + field(4)
         for h in range(2):
-            line = jnp.where(eye, loss[h * LANES : (h + 1) * LANES], 0.0)
-            loss_ref[pl.ds(2 * t + h, 1), :] = jnp.sum(line, axis=0, keepdims=True)
-        follow = split_dot(along, behind_ref[t]) + grad_trans * whole
+            turned_loss = loss[h * LANES : (h + 1) * LANES].T
+
+            @pl.when(has_first)
+            def _():
+                loss_ref[pl.ds(2 * t + h, 1), :] = turned_loss[:1]
+
+            @pl.when(has_last)
+            def _():
+                loss_ref[pl.ds(2 * t + 2 + h, 1), :] = turned_loss[LANES - 1 :]
+
+        follow = split_dot(along, to_right) + grad_trans * whole
         carry[...] = follow / through
 
         sums[...] = jnp.zeros_like(sums)
@@ -236,9 +293,9 @@
                 left[2] + right[2],
             ] + [sums[k * 9 + 6 + c] for c in range(3)]
             for n, value in enumerate(moments):
-                line = jnp.broadcast_to(jnp.sum(value, axis=0, keepdims=True), (8, LANES))
+                row = jnp.broadcast_to(jnp.sum(value, axis=0, keepdims=True), (8, LANES))
                 plain_sums[n] = (
-                    jnp.where(chosen, line, 0.0) if k == 0 else jnp.where(chosen, line, plain_sums[n])
+                    jnp.where(chosen, row, 0.0) if k == 0 else jnp.where(chosen, row, plain_sums[n])
                 )
         s0, su, sv, suu, suv, svv = plain_sums[:6]
         inv_scale = 1.0 / scale
@@ -255,14 +312,21 @@
             * (0.9 * (1.0 - curl * curl)),
             s0 * (1.0 - odds),
         ] + [plain_sums[6 + c] * tint[c] * (1.0 - tint[c]) for c in range(3)]
-        for p in range(9):
-            grads[pl.ds(pl.multiple_of(32 * p + 8 * t, 8), 8), :] = result[p]
-        return 0
+        for here, at in ((has_first, t), (has_last, t + 1)):
+
+            @pl.when(here)
+            def _():
+                place = places[at]
+                for p in range(9):
+                    value = jnp.take_along_axis(result[p], jnp.maximum(place, 0), axis=1)
+                    grads[pl.ds(pl.multiple_of(32 * p + 8 * at, 8), 8), :] = jnp.where(
+                        place >= 0, value, 0.0
+                    )
 
     grads[pl.ds(288, 96), :] = jnp.zeros((96, LANES), F32)
-    lax.fori_loop(0, 4, tile, 0)
+    lax.fori_loop(0, 4, block, 0)
     for b in range(3):
-        out_ref[:, b * LANES : (b + 1) * LANES] = grads[pl.ds(b * LANES, LANES), :].T
+        out_ref[pl.ds(b, LANES, stride=3), :] = grads[pl.ds(b * LANES, LANES), :].T
 
 
 def order_matrix(regions):
@@ -284,14 +348,20 @@
     my_index = lax.axis_index("region")
     limit = pltpu.CompilerParams(vmem_limit_bytes=32 * 1024 * 1024)
 
+    whole = pltpu.CompilerParams(vmem_limit_bytes=60 * 1024 * 1024)
+
+    def exchange(rows):
+        moved = lax.all_to_all(rows.reshape(regions, 1, WIDTH), "region", 0, 0, tiled=True)
+        return moved.reshape(rows.shape)
+
     message = pl.pallas_call(
         pack_kernel,
-        out_shape=jax.ShapeDtypeStruct((regions, WIDTH), F32),
-        scratch_shapes=[vmem(512, LANES), vmem(3, LANES, LANES)],
-        compiler_params=limit,
+        out_shape=jax.ShapeDtypeStruct((3 * regions, LANES), F32),
+        scratch_shapes=[vmem(512, LANES), vmem(LANES, LANES)],
+        compiler_params=whole,
         name="pack",
     )(gaussians.reshape(9, 32, LANES), depth[0].T, coverage)
-    received = lax.all_to_all(message, "region", 0, 0, tiled=True)
+    received = exchange(message)
 
     pix = pl.pallas_call(
         pixel_kernel,
@@ -317,16 +387,17 @@
     rank = jnp.arange(regions, dtype=F32)[None] + turned
     before = (rank[:, :, None] < rank[:, None, :]).astype(BF16)
     behind = (rank[:, :, None] > rank[:, None, :]).astype(BF16)
-    before = jnp.concatenate([before, jnp.ones_like(before)], 2)
 
     loss, returned = pl.pallas_call(
         splat_kernel,
         out_shape=(
             jax.ShapeDtypeStruct((8, LANES), F32),
-            jax.ShapeDtypeStruct((regions, WIDTH), F32),
+            jax.ShapeDtypeStruct((3 * regions, LANES), F32),
         ),
         scratch_shapes=[
             vmem(WIDTH, LANES),
+            vmem(4, 8, LANES, dtype=jnp.int32),
+            vmem(4, 8, LANES, dtype=jnp.int32),
             vmem(72, 8, LANES),
             vmem(SPLATS, 2, 3, 8, LANES),
             vmem(STEPS, SPLATS, 2 * ROWS, 8, LANES),
@@ -341,11 +412,10 @@
         name="splats",
     )(received, pix, before, behind)
 
-    back = lax.all_to_all(returned, "region", 0, 0, tiled=True)
+    back = exchange(returned)
     splat_grads = pl.pallas_call(
         unpack_kernel,
         out_shape=jax.ShapeDtypeStruct((9, 32, LANES), F32),
-        scratch_shapes=[vmem(3, LANES, LANES)],
         compiler_params=limit,
         name="unpack",
     )(back)

time: 51.6 us -> 47.3 us (0.917)
  local copies, waits for them, and re-layouts: 4.72 us -> 2.35 us
  Pallas kernels: 12.6 us -> 11.2 us
  waiting for transfers between devices: 6.13 us -> 4.92 us
  blocking collectives: 14.5 us -> 15.2 us
    pallas_call x1, Pallas kernels: 9.32 us -> 6.28 us  [shards(): pl.pallas_call(splat_kernel, out_shape=(jax.ShapeDtypeStruct((8, LANES),...]
    unnamed x20 -> x6, local copies, waits for them, and re-layouts: 3.63 us -> 0.98 us
    pallas_call x1, Pallas kernels: 0.34 us -> 2.01 us  [shards(): pl.pallas_call(pack_kernel, out_shape=jax.ShapeDtypeStruct((3 * regions,...]
    all_to_all x1, waiting for transfers between devices: 6.13 us -> 4.92 us  [exchange(): lax.all_to_all(rows.reshape(regions, 1, WIDTH), 'region', 0, 0, tiled=True)]
    all_to_all x2 -> x0, local copies, waits for them, and re-layouts: 1.08 us -> none  [the longest x1 0.88 us: shards(): received = lax.all_to_all(message, 'region', 0, 0, tiled=True)]
    broadcast_in_dim x1, local copies, waits for them, and re-layouts: 0.01 us -> 0.69 us  [shards(): b_first[None]]
    broadcast_in_dim x1, local copies, waits for them, and re-layouts: 0.01 us -> 0.68 us  [shards(): w_second[None]]
    all_to_all x1, blocking collectives: 14.5 us -> 15.2 us  [exchange(): lax.all_to_all(rows.reshape(regions, 1, WIDTH), 'region', 0, 0, tiled=True)]
  transfers between devices with their start and end apart: 1 -> 1, of which waited for: 1 -> 1; matrix products, arithmetic and copies ran while one was open for 2% -> 5% of each run, Pallas kernels for 4% -> 4%
where the time goes in v2:
time: 47.3 us; the launch traced here: 47 us
  blocking collectives  15.2 us (32%)
  starting transfers between devices  11.5 us (24%)
  Pallas kernels  11.2 us (24%)
  waiting for transfers between devices  4.92 us (10%)
  local copies, waits for them, and re-layouts  2.35 us (5%)
  matrix products  1.02 us (2%)
  between operations  0.69 us (1%)
    all_to_all x1, blocking collectives, exchange(): lax.all_to_all(rows.reshape(regions, 1, WIDTH), 'region', 0, 0, tiled=True)  15.2 us
    all_to_all x1, starting transfers between devices, exchange(): lax.all_to_all(rows.reshape(regions, 1, WIDTH), 'region', 0, 0, tiled=True)  11.5 us
    pallas_call x1, Pallas kernels, shards(): pl.pallas_call(splat_kernel, out_shape=(jax.ShapeDtypeStruct((8, LANES),...  6.28 us
    all_to_all x1, waiting for transfers between devices, exchange(): lax.all_to_all(rows.reshape(regions, 1, WIDTH), 'region', 0, 0, tiled=True)  4.92 us
    pallas_call x1, Pallas kernels, shards(): pl.pallas_call(pixel_kernel, grid=(4,), in_specs=[pl.BlockSpec((PIX, 384)...  2.08 us
    pallas_call x1, Pallas kernels, shards(): pl.pallas_call(pack_kernel, out_shape=jax.ShapeDtypeStruct((3 * regions,...  2.01 us
    dot_general x1, matrix products, shards(): jnp.dot(my_flips, jnp.asarray(order_matrix(regions)), precision=lax.Preci...  1.02 us
    unnamed x6, local copies, waits for them, and re-layouts  0.98 us
  transfers between devices with their start and end apart: 1, of which 1 were waited for; matrix products, arithmetic and copies ran while one was open for 5% of the time, Pallas kernels for 4%

profile of v2, /device:TPU:1, one launch (start us, length us, event | category | flops | bytes accessed | tf_op | source)
XLA Modules:
  0.0 47.0 jit_solution(8606715113523915281)
XLA Ops:
  0.6 0.0 copy-start
  0.6 2.0 %pack.1 = f32[384,128]{1,0:T(8,128)} custom-call(f32[9,32,128]{2,1,0:T(8,128)} %bitcast.15, s32[8,512]{1,0:T(8,128)} %bitcast.17, s32[1,512]{1,0:T(1,128)} %cover_ref.1), custom_call_target="tpu_custom_call" | custom-call | tf_op jit(solution)/shard_map/pack/pallas_call | solution.py:357
  2.6 11.5 %all-to-all-start = ((f32[128,1,384]{2,1,0:T(1,128)}), f32[128,1,384]{2,1,0:T(1,128)S(1)}, u32[]{:S(2)}, u32[]{:S(2)}) async-start(f32[128,1,384]{2,1,0:T(1,128)} %bitcast.14), calls=%async_computation | async-start | bytes 393216 | tf_op jit(solution)/shard_map/all_to_all | solution.py:354
  14.2 0.7 %broadcast_in_dim.4.b_first_ref = f32[1,384]{1,0:T(1,128)S(1)} reshape(f32[384]{0:T(512)} %param.16) | data formatting | bytes 3072 | tf_op jit(solution)/shard_map/broadcast_in_dim | solution.py:383
  14.8 0.7 %broadcast_in_dim.5.w_second_ref = bf16[1,384]{1,0:T(2,128)(2,1)S(1)} reshape(bf16[384]{0:T(512)(128)(2,1)} %param.17) | data formatting | bytes 1536 | tf_op jit(solution)/shard_map/broadcast_in_dim | solution.py:383
  15.5 0.0 copy-start.2
  15.5 1.0 %convolution_add_fusion = f32[4,128]{1,0:T(4,128)S(1)} fusion(f32[127,128]{1,0:T(8,128)} %constant.12.clone, s32[512,127]{1,0:T(8,128)} %param.13, s32[]{:T(128)S(6)} %select_n.3), kind=kOutput, calls=%fused_computation | convolution fusion | flops 781308 | bytes 69636 | tf_op jit(solution)/shard_map/dot_general | solution.py:386
  16.5 0.0 copy-done
  16.6 0.0 copy-done.2
  16.6 0.0 copy-start.1
  16.6 1.0 %copy-done.1 = bf16[384,384]{1,0:T(8,128)(2,1)S(1)} copy-done((bf16[384,384]{1,0:T(8,128)(2,1)S(1)}, bf16[384,384]{1,0:T(8,128)(2,1)}, u32[]{:S(2)}) %copy-start.1) | copy-done | bytes 294936
  17.5 2.1 %pixels.1.pix_ref = f32[1024,128]{1,0:T(8,128)S(1)} custom-call(bf16[1024,384]{1,0:T(8,128)(2,1)S(1)} %copy-done, bf16[384,384]{1,0:T(8,128)(2,1)S(1)} %copy-done.1, f32[1,384]{1,0:T(1,128)S(1)} %broadcast_in_dim.4.b_first_ref, bf16[1,384]{1,0:T(2,128)(2,1)S(1)} %broadcast_in_dim.5.w_second_ref, f32[3,1024]{1,0:T(4,128)S(1)} %copy-done.2), custom_call_target="tpu_custom_call" | custom-call | flops 402653184 | bytes 2000000 | tf_op jit(solution)/shard_map/pixels/pallas_call | solution.py:366
  19.6 0.1 compare_convert_fusion
  19.8 4.9 %all-to-all-done = f32[128,1,384]{2,1,0:T(1,128)S(1)} async-done(((f32[128,1,384]{2,1,0:T(1,128)}), f32[128,1,384]{2,1,0:T(1,128)S(1)}, u32[]{:S(2)}, u32[]{:S(2)}) %all-to-all-start) | async-done | bytes 196640 | tf_op jit(solution)/shard_map/all_to_all | solution.py:354
  24.7 6.3 %splats.1 = (f32[8,128]{1,0:T(8,128)}, f32[384,128]{1,0:T(8,128)S(1)}) custom-call(f32[384,128]{1,0:T(8,128)S(1)} %bitcast.12, f32[1024,128]{1,0:T(8,128)S(1)} %pixels.1.pix_ref, bf16[4,128,128]{2,1,0:T(8,128)(2,1)S(1)} %get-tuple-element.13.before_ref, bf16[4,128,128]{2,1,0:T(8,128)(2,1)S(1)} %get-tuple-element.12.behind_ref), custom_call_target="tpu_custom_call" | custom-call | tf_op jit(solution)/shard_map/splats/pallas_call | solution.py:391
  31.0 15.2 %all_to_all.10 = f32[128,1,384]{2,1,0:T(1,128)S(1)} all-to-all(f32[128,1,384]{2,1,0:T(1,128)S(1)} %bitcast.13), channel_id=1, replica_groups=mesh['region'=128] {'region'}, dimensions={0} | all-to-all | bytes 393216 | tf_op jit(solution)/shard_map/all_to_all | solution.py:354
  46.2 0.8 %unpack.1 = f32[9,32,128]{2,1,0:T(8,128)} custom-call(f32[384,128]{1,0:T(8,128)S(1)} %bitcast.11), custom_call_target="tpu_custom_call" | custom-call | tf_op jit(solution)/shard_map/unpack/pallas_call | solution.py:416
Async XLA Ops:
  0.6 15.9 %copy-start = (bf16[1024,384]{1,0:T(8,128)(2,1)S(1)}, bf16[1024,384]{1,0:T(8,128)(2,1)}, u32[]{:S(2)}) copy-start(bf16[1024,384]{1,0:T(8,128)(2,1)} %feat_ref.1) | copy-start | bytes 2359300
  2.6 22.0 %all-to-all-start = ((f32[128,1,384]{2,1,0:T(1,128)}), f32[128,1,384]{2,1,0:T(1,128)S(1)}, u32[]{:S(2)}, u32[]{:S(2)}) async-start(f32[128,1,384]{2,1,0:T(1,128)} %bitcast.14), calls=%async_computation | async-start | bytes 393216 | tf_op jit(solution)/shard_map/all_to_all | solution.py:354
  15.5 1.0 %copy-start.2 = (f32[3,1024]{1,0:T(4,128)S(1)}, f32[3,1024]{1,0:T(4,128)}, u32[]{:S(2)}) copy-start(f32[3,1024]{1,0:T(4,128)} %target_ref.1) | copy-start | bytes 36868
  16.6 1.0 %copy-start.1 = (bf16[384,384]{1,0:T(8,128)(2,1)S(1)}, bf16[384,384]{1,0:T(8,128)(2,1)}, u32[]{:S(2)}) copy-start(bf16[384,384]{1,0:T(8,128)(2,1)} %w_first_ref.1) | copy-start | bytes 884740

commit v3 on v2

v3 whole, which is shorter than its diff:
```python
import math

import jax
import jax.numpy as jnp
import numpy as np
from jax import lax
from jax.experimental import pallas as pl
from jax.experimental.pallas import tpu as pltpu
from jax.sharding import PartitionSpec as P

TSIDE = 16
PIX = TSIDE * TSIDE
SPLATS = 8
LANES = 128
WIDTH = 384
HALF_LOG2E = 0.5 * math.log2(math.e)
F32 = jnp.float32
BF16 = jnp.bfloat16


def cut_columns(source, shift):
    return pltpu.roll(source, shift, 1) if shift else source


def pack_kernel(gauss_ref, depth_ref, cover_ref, out_ref, turned, strided):
    group = lax.broadcasted_iota(jnp.int32, (32, LANES), 1) // 32
    for part in range(3):
        for d in range(4):
            block = None
            for a in range(min(4, 9 - 4 * part)):
                moved = cut_columns(gauss_ref[4 * part + a], 32 * ((a - d) % 4))
                block = moved if block is None else jnp.where(group == a, moved, block)
            if part < 2:
                out_ref[pl.ds(3 * d + part, 32, stride=12), :] = block
            else:
                strided[pl.ds(d, 32, stride=4), :] = block
    ranks = depth_ref[...].astype(F32)
    covered = cover_ref[...].astype(F32)
    filler = jnp.zeros((LANES - 16, 512), F32)
    row = lax.broadcasted_iota(jnp.int32, (8, 512), 0)
    covered = jnp.where(row == 0, jnp.broadcast_to(covered, (8, 512)), 0.0)
    stacked = jnp.concatenate([ranks, covered, filler], 0)
    for b in range(4):
        turned[pl.ds(b * LANES, LANES), :] = stacked[:, b * LANES : (b + 1) * LANES].T
    tail = None
    for t in range(4):
        moved = pltpu.roll(turned[pl.ds(t, LANES, stride=4), :], 32 + 16 * t, 1)
        tail = moved if tail is None else tail + moved
    lane = lax.broadcasted_iota(jnp.int32, (LANES, LANES), 1)
    out_ref[pl.ds(2, LANES, stride=3), :] = jnp.where(lane < 32, strided[...], tail)


def unpack_kernel(msg_ref, out_ref):
    group = lax.broadcasted_iota(jnp.int32, (32, LANES), 1) // 32
    for p in range(9):
        a, part = p % 4, p // 4
        block = None
        for d in range(4):
            moved = cut_columns(msg_ref[pl.ds(3 * d + part, 32, stride=12), :], 32 * ((d - a) % 4))
            block = moved if block is None else jnp.where(group == d, moved, block)
        out_ref[p] = block


def pixel_kernel(
    w_first_hbm, b_first_hbm, w_second_hbm, feat_hbm, target_hbm, flips_hbm, turns_hbm,
    pix_ref, before_ref, behind_ref,
    w_first_ref, b_first_ref, w_second_ref, feat_ref, target_ref, flips_ref, turns_ref, arrived,
):
    me = lax.axis_index("region")
    first_row = pl.multiple_of(8 * (me // 2), 8)
    pairs = [
        (w_first_hbm, w_first_ref),
        (b_first_hbm, b_first_ref),
        (w_second_hbm, w_second_ref),
        (target_hbm, target_ref),
        (flips_hbm.at[pl.ds(first_row, 8), :], flips_ref),
        (turns_hbm, turns_ref),
    ] + [(feat_hbm.at[pl.ds(t * PIX, PIX), :], feat_ref.at[pl.ds(t * PIX, PIX), :]) for t in range(4)]
    fetches = [
        pltpu.make_async_copy(source, landing, arrived.at[n])
        for n, (source, landing) in enumerate(pairs)
    ]
    for fetch in fetches:
        fetch.start()
    for fetch in fetches[:6]:
        fetch.wait()
    rows = jnp.broadcast_to(w_second_ref[...][None, :], (LANES, w_second_ref.shape[0]))
    bias = b_first_ref[...][None, :]
    lane = lax.broadcasted_iota(jnp.int32, (PIX, LANES), 1)
    filler = jnp.zeros((LANES - 3, PIX), F32)
    for t in range(4):
        fetches[6 + t].wait()
        at = pl.ds(t * PIX, PIX)
        pre = jnp.dot(feat_ref[at, :], w_first_ref[...], preferred_element_type=F32) + bias
        hidden = jax.nn.gelu(pre).astype(BF16)
        score = lax.dot_general(
            hidden, rows, (((1,), (1,)), ((), ())), preferred_element_type=F32
        )
        spread = 0.5 + (jnp.maximum(score, 0.0) + jnp.log1p(jnp.exp(-jnp.abs(score))))
        wanted = jnp.concatenate([target_ref[:, t * PIX : (t + 1) * PIX], filler], 0).T
        pix_ref[at, :] = jnp.where(
            lane == 3, 1.0 / (spread * spread), jnp.where(lane == 4, jnp.log(spread), wanted)
        )
    turned = jnp.dot(
        flips_ref[...].astype(F32).astype(BF16), turns_ref[...], preferred_element_type=F32
    )
    ranks = jnp.where(me % 2 == 0, turned[:4], turned[4:])
    ranks = ranks + lax.broadcasted_iota(jnp.int32, (4, LANES), 1).astype(F32)
    for t in range(4):
        across = jnp.broadcast_to(ranks[t : t + 1], (LANES, LANES))
        down = across.T
        before_ref[t] = jnp.where(down < across, 1.0, 0.0).astype(BF16)
        behind_ref[t] = jnp.where(down > across, 1.0, 0.0).astype(BF16)


def split_dot(value, matrix):
    high = value.astype(BF16)
    low = (value - high.astype(F32)).astype(BF16)
    return jnp.dot(high, matrix, preferred_element_type=F32) + jnp.dot(
        low, matrix, preferred_element_type=F32
    )


ROWS = 4
STEPS = TSIDE // ROWS


def splat_kernel(
    msg_ref, pix_ref, before_ref, behind_ref, loss_ref, out_ref,
    turned, places, sources, rows, across, alphas, weights, clear, color, carry, sums, grads,
):
    last_part = msg_ref[pl.ds(2, LANES, stride=3), :]
    turned[pl.ds(2 * LANES, LANES), :] = last_part.T
    for b in range(2):
        turned[pl.ds(b * LANES, LANES), :] = msg_ref[pl.ds(b, LANES, stride=3), :].T
    sub = lax.broadcasted_iota(jnp.int32, (8, LANES), 0).astype(F32)
    lane = lax.broadcasted_iota(jnp.int32, (LANES, LANES), 1)
    line = lax.broadcasted_iota(jnp.int32, (LANES, LANES), 0)
    loss_ref[...] = jnp.zeros_like(loss_ref)
    grads[...] = jnp.zeros_like(grads)

    counts = []
    for t in range(4):
        kept = jnp.where(lane[:8] == 0, 1.0, turned[pl.ds(288 + 16 * t + 8, 1), :])
        kept_down = jnp.where(line == 0, 1.0, last_part[:, 32 + 16 * t + 8 : 32 + 16 * t + 9])
        counts.append(jnp.sum(kept[:1]).astype(jnp.int32))
        if t % 2 == 0:
            ahead_of, ahead_down = before_ref[t], behind_ref[t]
        else:
            ahead_of, ahead_down = behind_ref[t], before_ref[t]
        spot = jnp.dot(kept.astype(BF16), ahead_of, preferred_element_type=F32)
        spot_down = jnp.dot(ahead_down, kept_down.astype(BF16), preferred_element_type=F32)
        if t % 2 == 1:
            spot, spot_down = (LANES - 1.0) - spot, (LANES - 1.0) - spot_down
        places[t] = jnp.where(kept > 0.0, spot, -1.0).astype(jnp.int32)
        hit = jnp.logical_and(kept_down > 0.0, spot_down == lane.astype(F32))
        source = jnp.sum(jnp.where(hit, line.astype(F32), 0.0), axis=0, keepdims=True)
        sources[t] = jnp.broadcast_to(source, (8, LANES)).astype(jnp.int32)

    fits = [counts[2 * s] + counts[2 * s + 1] <= LANES for s in range(2)]

    def unit_y(s, k, step, r):
        at = (step * ROWS + r).astype(F32) + 0.5
        return (at - rows[s, k * 9 + 1]) * rows[s, k * 9 + 3]

    def render(step, unused):
        for s in range(2):
            trans = [[None] * 2 for _ in range(ROWS)]
            total = [[[None] * 3 for _ in range(2)] for _ in range(ROWS)]
            for k in range(SPLATS):
                shade = [rows[s, k * 9 + 6 + c] for c in range(3)]
                for r in range(ROWS):
                    down = unit_y(s, k, step, r)
                    for h in range(2):
                        power = down * (across[s, k, h, 1] - down) - across[s, k, h, 2]
                        alpha = jnp.exp2(power)
                        weight = alpha if k == 0 else trans[r][h] * alpha
                        trans[r][h] = 1.0 - alpha if k == 0 else trans[r][h] - weight
                        alphas[s, step, k, 2 * r + h] = alpha
                        weights[s, step, k, 2 * r + h] = weight
                        for c in range(3):
                            term = weight * shade[c]
                            total[r][h][c] = term if k == 0 else total[r][h][c] + term
            for r in range(ROWS):
                for h in range(2):
                    at = pl.ds(pl.multiple_of((step * ROWS + r) * 16 + 8 * h, 8), 8)
                    clear[s, at, :] = trans[r][h]
                    for c in range(3):
                        color[s, c, at, :] = total[r][h][c]
        return 0

    def pull(step, unused):
        for s in range(2):
            behind = [None] * (2 * ROWS)
            slope = [[None] * 3 for _ in range(2 * ROWS)]
            for n in range(2 * ROWS):
                at = pl.ds(pl.multiple_of(step * (ROWS * 16) + 8 * n, 8), 8)
                behind[n] = carry[s, at, :]
                slope[n] = [color[s, c, at, :] for c in range(3)]
            for k in range(SPLATS - 1, -1, -1):
                shade = [rows[s, k * 9 + 6 + c] for c in range(3)]
                acc = [None] * 9

                def add(n, value):
                    acc[n] = value if acc[n] is None else acc[n] + value

                for r in range(ROWS):
                    down = unit_y(s, k, step, r)
                    for h in range(2):
                        n = 2 * r + h
                        alpha = alphas[s, step, k, n]
                        weight = weights[s, step, k, n]
                        gain = slope[n][0] * shade[0] + slope[n][1] * shade[1] + slope[n][2] * shade[2]
                        change = gain - behind[n]
                        behind[n] = behind[n] + alpha * change
                        pulled = weight * change
                        leaned = pulled * down
                        add(3 * h, pulled)
                        add(3 * h + 1, leaned)
                        add(3 * h + 2, leaned * down)
                        for c in range(3):
                            add(6 + c, weight * slope[n][c])
                for n in range(9):
                    sums[s, k * 9 + n] = sums[s, k * 9 + n] + acc[n]
        return 0

    def constants(s, has_first, has_last):
        t = 2 * s
        flat = lane[:8]
        in_first = flat < jnp.where(has_first, counts[t], 0)
        in_last = flat >= jnp.where(has_last, LANES - counts[t + 1], LANES)
        first_source, last_source = sources[t], sources[t + 1]

        def pick(at, step, empty=0.0):
            left = jnp.take_along_axis(turned[pl.ds(at, 8), :], first_source, axis=1)
            right = jnp.take_along_axis(turned[pl.ds(at + step, 8), :], last_source, axis=1)
            return jnp.where(in_first, left, jnp.where(in_last, right, empty))

        raw = [pick(32 * p + 8 * t, 8) for p in range(9)]
        ranks = pick(288 + 16 * t, 16, sub)
        covered = pick(288 + 16 * t + 8, 16)[:1]
        inv_x = jnp.exp(-raw[2])
        inv_y = jnp.exp(-raw[3])
        curl = jnp.tanh(raw[4])
        rho = 0.9 * curl
        inv_det = 1.0 / (1.0 - rho * rho)
        scale = jnp.sqrt(HALF_LOG2E * inv_det)
        odds = jax.nn.sigmoid(raw[5])
        tint = [jax.nn.sigmoid(raw[6 + c]) for c in range(3)]
        opacity = 0.99 * odds * covered
        faint = jnp.where(opacity > 0.0, jnp.log2(jnp.maximum(opacity, 1.1754944e-38)), -1e30)
        plain = [raw[0], raw[1], inv_x * scale, inv_y * scale, 2.0 * rho, faint] + tint
        return ranks, inv_x, inv_y, curl, rho, inv_det, scale, odds, tint, plain

    def prepare(s, ranks, plain):
        for k in range(SPLATS):
            chosen = ranks == float(k)
            for n, value in enumerate(plain):
                row = jnp.sum(jnp.where(chosen, value, 0.0), axis=0, keepdims=True)
                rows[s, k * 9 + n] = jnp.broadcast_to(row, (8, LANES))
            for h in range(2):
                unit = (sub + (0.5 + 8.0 * h) - rows[s, k * 9]) * rows[s, k * 9 + 2]
                across[s, k, h, 0] = unit
                across[s, k, h, 1] = unit * rows[s, k * 9 + 4]
                across[s, k, h, 2] = unit * unit - rows[s, k * 9 + 5]

    on_lane = lax.broadcasted_iota(jnp.int32, (PIX, LANES), 1)

    def composite(flags):
        borders, logs, sames, rights = [], [], [], []
        for s, (has_first, has_last) in enumerate(flags):
            border = jnp.where(has_first, jnp.where(has_last, counts[2 * s], LANES), 0)
            same = (lane < border) == (line < border)
            left = jnp.where(jnp.logical_and(same, line < lane), 1.0, 0.0).astype(BF16)
            rights.append(jnp.where(jnp.logical_and(same, line > lane), 1.0, 0.0).astype(BF16))
            sames.append(jnp.where(same, 1.0, 0.0).astype(BF16))
            borders.append(border)
            logs.append(split_dot(jnp.log(clear[s]), jnp.concatenate([left, sames[s]], 1)))
        losses = []
        alongs, grad_transes = [], []
        for s in range(2):
            ahead = jnp.exp(logs[s][:, :LANES])
            whole = jnp.exp(logs[s][:, LANES:])
            left_pix = pix_ref[pl.ds(2 * s * PIX, PIX), :]
            right_pix = pix_ref[pl.ds((2 * s + 1) * PIX, PIX), :]
            on_left = on_lane < borders[s]

            def field(n):
                return jnp.where(on_left, left_pix[:, n : n + 1], right_pix[:, n : n + 1])

            inv_square = field(3)
            squares = None
            grad_trans = None
            along = None
            for c in range(3):
                layer = ahead * color[s, c]
                residual = split_dot(layer, sames[s]) + whole - field(c)
                slope = residual * inv_square
                squares = residual * residual if c == 0 else squares + residual * residual
                grad_trans = slope if c == 0 else grad_trans + slope
                along = slope * layer if c == 0 else along + slope * layer
                color[s, c] = ahead * slope
            losses.append(0.5 * squares * inv_square + field(4))
            alongs.append(along)
            grad_transes.append(grad_trans * whole)
        for s, (has_first, has_last) in enumerate(flags):
            follow = split_dot(alongs[s], rights[s]) + grad_transes[s]
            carry[s] = follow / clear[s]
        for s, (has_first, has_last) in enumerate(flags):
            for h in range(2):
                shown = losses[s][h * LANES : (h + 1) * LANES].T
                for here, row, value in (
                    (has_first, 4 * s + h, shown[:1]),
                    (has_last, 4 * s + 2 + h, shown[LANES - 1 :]),
                ):
                    loss_ref[row : row + 1, :] = jnp.where(here, value, loss_ref[row : row + 1, :])

    def finish(s, flag, ranks, inv_x, inv_y, curl, rho, inv_det, scale, odds, tint):
        plain_sums = [None] * 9
        for k in range(SPLATS):
            chosen = ranks == float(k)
            left, right = [[sums[s, k * 9 + 3 * h + n] for n in range(3)] for h in range(2)]
            u0, u1 = across[s, k, 0, 0], across[s, k, 1, 0]
            m0, m1 = left[0] * u0, right[0] * u1
            moments = [
                left[0] + right[0],
                m0 + m1,
                left[1] + right[1],
                m0 * u0 + m1 * u1,
                left[1] * u0 + right[1] * u1,
                left[2] + right[2],
            ] + [sums[s, k * 9 + 6 + c] for c in range(3)]
            for n, value in enumerate(moments):
                row = jnp.broadcast_to(jnp.sum(value, axis=0, keepdims=True), (8, LANES))
                plain_sums[n] = (
                    jnp.where(chosen, row, 0.0) if k == 0 else jnp.where(chosen, row, plain_sums[n])
                )
        s0, su, sv, suu, suv, svv = plain_sums[:6]
        inv_scale = 1.0 / scale
        su, sv = su * inv_scale, sv * inv_scale
        inv_both = inv_scale * inv_scale
        suu, suv, svv = suu * inv_both, suv * inv_both, svv * inv_both
        result = [
            inv_det * inv_x * (su - rho * sv),
            inv_det * inv_y * (sv - rho * su),
            inv_det * (suu - rho * suv),
            inv_det * (svv - rho * suv),
            inv_det
            * (suv - rho * inv_det * (suu - 2.0 * rho * suv + svv))
            * (0.9 * (1.0 - curl * curl)),
            s0 * (1.0 - odds),
        ] + [plain_sums[6 + c] * tint[c] * (1.0 - tint[c]) for c in range(3)]
        for here, t in zip(flag, (2 * s, 2 * s + 1)):
            place = places[t]
            taken = jnp.logical_and(place >= 0, here)
            place = jnp.maximum(place, 0)
            for p in range(9):
                at = pl.ds(32 * p + 8 * t, 8)
                value = jnp.take_along_axis(result[p], place, axis=1)
                grads[at, :] = jnp.where(taken, value, grads[at, :])

    def both_blocks(turn, unused):
        opening = turn == 0
        flags = [(opening, jnp.logical_xor(fits[s], turn == 1)) for s in range(2)]
        held = [constants(s, *flags[s]) for s in range(2)]
        for s in range(2):
            prepare(s, held[s][0], held[s][-1])
        lax.fori_loop(0, STEPS, render, 0)
        composite(flags)
        sums[...] = jnp.zeros_like(sums)
        lax.fori_loop(0, STEPS, pull, 0)
        for s in range(2):
            finish(s, flags[s], *held[s][:-1])
        return 0

    turns = jnp.where(jnp.logical_and(fits[0], fits[1]), 1, 2)
    lax.fori_loop(0, turns, both_blocks, 0)
    for b in range(3):
        out_ref[pl.ds(b, LANES, stride=3), :] = grads[pl.ds(b * LANES, LANES), :].T


def order_matrix(regions):
    levels = regions.bit_length() - 1
    turns = np.zeros((regions - 1, regions), np.float32)
    for r in range(regions):
        for d in range(levels):
            bit = (r >> (levels - 1 - d)) & 1
            turns[2**d - 1 + (r >> (levels - d)), r] = (1 - 2 * bit) * 2 ** (levels - 1 - d)
    return turns


def vmem(*shape, dtype=F32):
    return pltpu.VMEM(shape, dtype)


def shards(gaussians, depth, coverage, flips, features, w_first, b_first, w_second, target):
    regions = lax.axis_size("region")
    my_index = lax.axis_index("region")
    limit = pltpu.CompilerParams(vmem_limit_bytes=32 * 1024 * 1024)

    whole = pltpu.CompilerParams(vmem_limit_bytes=60 * 1024 * 1024)

    def exchange(rows):
        moved = lax.all_to_all(rows.reshape(regions, 1, WIDTH), "region", 0, 0, tiled=True)
        return moved.reshape(rows.shape)

    message = pl.pallas_call(
        pack_kernel,
        out_shape=jax.ShapeDtypeStruct((3 * regions, LANES), F32),
        scratch_shapes=[vmem(512, LANES), vmem(LANES, LANES)],
        compiler_params=whole,
        name="pack",
    )(gaussians.reshape(9, 32, LANES), depth[0].T, coverage)
    received = exchange(message)

    order = jax.ShapeDtypeStruct((4, LANES, LANES), BF16)
    operands = (
        w_first, b_first, w_second, features, target, flips, jnp.asarray(order_matrix(regions), BF16)
    )
    landings = [pltpu.VMEM(x.shape, x.dtype) for x in operands]
    landings[5] = pltpu.VMEM((8, regions - 1), jnp.int32)
    pix, before, behind = pl.pallas_call(
        pixel_kernel,
        in_specs=[pl.BlockSpec(memory_space=pltpu.HBM)] * 7,
        out_shape=(jax.ShapeDtypeStruct((4 * PIX, LANES), F32), order, order),
        scratch_shapes=landings + [pltpu.SemaphoreType.DMA((10,))],
        compiler_params=limit,
        cost_estimate=pl.CostEstimate(
            flops=2 * 1024 * 384 * 512, bytes_accessed=2_000_000, transcendentals=1024 * 384
        ),
        name="pixels",
    )(*operands)

    loss, returned = pl.pallas_call(
        splat_kernel,
        out_shape=(
            jax.ShapeDtypeStruct((8, LANES), F32),
            jax.ShapeDtypeStruct((3 * regions, LANES), F32),
        ),
        scratch_shapes=[
            vmem(WIDTH, LANES),
            vmem(4, 8, LANES, dtype=jnp.int32),
            vmem(4, 8, LANES, dtype=jnp.int32),
            vmem(2, 72, 8, LANES),
            vmem(2, SPLATS, 2, 3, 8, LANES),
            vmem(2, STEPS, SPLATS, 2 * ROWS, 8, LANES),
            vmem(2, STEPS, SPLATS, 2 * ROWS, 8, LANES),
            vmem(2, PIX, LANES),
            vmem(2, 3, PIX, LANES),
            vmem(2, PIX, LANES),
            vmem(2, 72, 8, LANES),
            vmem(WIDTH, LANES),
        ],
        compiler_params=limit,
        name="splats",
    )(received, pix, before, behind)

    back = exchange(returned)
    splat_grads = pl.pallas_call(
        unpack_kernel,
        out_shape=jax.ShapeDtypeStruct((9, 32, LANES), F32),
        compiler_params=limit,
        name="unpack",
    )(back)
    return loss.reshape(4 * PIX), splat_grads.reshape(1, 9, 32 * LANES)


def solution(mesh):
    placed = (
        P("region", None, None),
        P("region", None, None),
        P("region", None),
        P(),
        P("region", None),
        P(),
        P(),
        P(),
        P(None, "region"),
    )
    return jax.shard_map(
        shards,
        mesh=mesh,
        in_specs=placed,
        out_specs=(P("region"), P("region", None, None)),
        check_vma=False,
    )
```

time: 47.3 us -> 45 us (0.951)
  local copies, waits for them, and re-layouts: 2.35 us -> 1.15 us
  waiting for transfers between devices: 4.92 us -> 5.96 us
  matrix products: 1.02 us -> 0 us
  blocking collectives: 15.2 us -> 14.5 us
    pallas_call x1, Pallas kernels: 6.28 us -> 4.68 us  [shards(): pl.pallas_call(splat_kernel, out_shape=(jax.ShapeDtypeStruct((8, LANES),...]
    broadcast_in_dim x2 -> x0, local copies, waits for them, and re-layouts: 1.37 us -> none  [the longest x1 0.69 us: shards(): b_first[None]]
    pallas_call x1, Pallas kernels: 2.08 us -> 3.37 us  [shards(): pl.pallas_call(pixel_kernel, in_specs=[pl.BlockSpec(memory_space=pltpu.HB...]
    all_to_all x1, waiting for transfers between devices: 4.92 us -> 5.96 us  [exchange(): lax.all_to_all(rows.reshape(regions, 1, WIDTH), 'region', 0, 0, tiled=True)]
    dot_general x1 -> x0, matrix products: 1.02 us -> none  [shards(): jnp.dot(my_flips, jnp.asarray(order_matrix(regions)), precision=lax.Preci...]
    all_to_all x1, blocking collectives: 15.2 us -> 14.5 us  [exchange(): lax.all_to_all(rows.reshape(regions, 1, WIDTH), 'region', 0, 0, tiled=True)]
    unnamed x6 -> x14, local copies, waits for them, and re-layouts: 0.98 us -> 1.15 us
  transfers between devices with their start and end apart: 1 -> 1, of which waited for: 1 -> 1; matrix products, arithmetic and copies ran while one was open for 5% -> 0% of each run, Pallas kernels for 4% -> 8%
where the time goes in v3:
time: 45 us; the launch traced here: 44.8 us
  blocking collectives  14.5 us (32%)
  starting transfers between devices  11.5 us (26%)
  Pallas kernels  10.9 us (24%)
  waiting for transfers between devices  5.96 us (13%)
  local copies, waits for them, and re-layouts  1.15 us (3%)
  between operations  0.73 us (2%)
    all_to_all x1, blocking collectives, exchange(): lax.all_to_all(rows.reshape(regions, 1, WIDTH), 'region', 0, 0, tiled=True)  14.5 us
    all_to_all x1, starting transfers between devices, exchange(): lax.all_to_all(rows.reshape(regions, 1, WIDTH), 'region', 0, 0, tiled=True)  11.5 us
    all_to_all x1, waiting for transfers between devices, exchange(): lax.all_to_all(rows.reshape(regions, 1, WIDTH), 'region', 0, 0, tiled=True)  5.96 us
    pallas_call x1, Pallas kernels, shards(): pl.pallas_call(splat_kernel, out_shape=(jax.ShapeDtypeStruct((8, LANES),...  4.68 us
    pallas_call x1, Pallas kernels, shards(): pl.pallas_call(pixel_kernel, in_specs=[pl.BlockSpec(memory_space=pltpu.HB...  3.37 us
    pallas_call x1, Pallas kernels, shards(): pl.pallas_call(pack_kernel, out_shape=jax.ShapeDtypeStruct((3 * regions,...  1.99 us
    unnamed x14, local copies, waits for them, and re-layouts  1.15 us
  transfers between devices with their start and end apart: 1, of which 1 were waited for; matrix products, arithmetic and copies ran while one was open for 0% of the time, Pallas kernels for 8%

profile of v3, /device:TPU:1, one launch (start us, length us, event | category | flops | bytes accessed | tf_op | source)
XLA Modules:
  0.0 44.8 jit_solution(16949308540396259029)
XLA Ops:
  0.6 0.0 copy-start.1
  0.6 2.0 %pack.1 = f32[384,128]{1,0:T(8,128)} custom-call(f32[9,32,128]{2,1,0:T(8,128)} %bitcast.14, s32[8,512]{1,0:T(8,128)} %bitcast.16, s32[1,512]{1,0:T(1,128)} %cover_ref.1), custom_call_target="tpu_custom_call" | custom-call | tf_op jit(solution)/shard_map/pack/pallas_call | solution.py:407
  2.6 0.0 copy-start.2
  2.6 0.0 copy-start.3
  2.6 0.0 copy-start.4
  2.6 0.0 copy-start.5
  2.6 0.0 copy-start.6
  2.7 11.5 %all-to-all-start = ((f32[128,1,384]{2,1,0:T(1,128)}), f32[128,1,384]{2,1,0:T(1,128)S(1)}, u32[]{:S(2)}, u32[]{:S(2)}) async-start(f32[128,1,384]{2,1,0:T(1,128)} %bitcast.13), calls=%async_computation | async-start | bytes 393216 | tf_op jit(solution)/shard_map/all_to_all | solution.py:404
  14.2 0.0 copy-done.1
  14.2 0.0 copy-done.2
  14.2 0.0 copy-done.3
  14.2 0.0 copy-done.4
  14.2 0.0 copy-done.5
  14.2 0.0 copy-done.6
  14.2 0.0 copy-start
  14.2 1.1 %copy-done = bf16[1024,384]{1,0:T(8,128)(2,1)S(1)} copy-done((bf16[1024,384]{1,0:T(8,128)(2,1)S(1)}, bf16[1024,384]{1,0:T(8,128)(2,1)}, u32[]{:S(2)}) %copy-start) | copy-done | bytes 786456
  15.4 3.4 %pixels.1 = (f32[1024,128]{1,0:T(8,128)S(1)}, bf16[4,128,128]{2,1,0:T(8,128)(2,1)S(1)}, bf16[4,128,128]{2,1,0:T(8,128)(2,1)S(1)}) custom-call(bf16[384,384]{1,0:T(8,128)(2,1)S(1)} %copy-done.1, f32[384]{0:T(512)S(1)} %copy-done.4, bf16[384]{0:T(512)(128)(2,1)S(1)} %copy-done.5, bf16[1024,384]{1,0:T(8,128)(2,1)S(1)} %copy-done, f32[3,1024]{1,0:T(4,128)S(1)} %copy-done.3, ...), custom_call_target="tpu_custom_call" | custom-call | flops 402653184 | bytes 2000000 | tf_op jit(solution)/shard_map/pixels/pallas_call | solution.py:422
  18.7 6.0 %all-to-all-done = f32[128,1,384]{2,1,0:T(1,128)S(1)} async-done(((f32[128,1,384]{2,1,0:T(1,128)}), f32[128,1,384]{2,1,0:T(1,128)S(1)}, u32[]{:S(2)}, u32[]{:S(2)}) %all-to-all-start) | async-done | bytes 196640 | tf_op jit(solution)/shard_map/all_to_all | solution.py:404
  24.7 4.7 %splats.1 = (f32[8,128]{1,0:T(8,128)}, f32[384,128]{1,0:T(8,128)S(1)}) custom-call(f32[384,128]{1,0:T(8,128)S(1)} %bitcast.11, f32[1024,128]{1,0:T(8,128)S(1)} %get-tuple-element.7.pix_ref, bf16[4,128,128]{2,1,0:T(8,128)(2,1)S(1)} %get-tuple-element.8.before_ref, bf16[4,128,128]{2,1,0:T(8,128)(2,1)S(1)} %get-tuple-element.9.behind_ref), custom_call_target="tpu_custom_call" | custom-call | tf_op jit(solution)/shard_map/splats/pallas_call | solution.py:434
  29.4 14.5 %all_to_all.10 = f32[128,1,384]{2,1,0:T(1,128)S(1)} all-to-all(f32[128,1,384]{2,1,0:T(1,128)S(1)} %bitcast.12), channel_id=1, replica_groups=mesh['region'=128] {'region'}, dimensions={0} | all-to-all | bytes 393216 | tf_op jit(solution)/shard_map/all_to_all | solution.py:404
  43.9 0.8 %unpack.1 = f32[9,32,128]{2,1,0:T(8,128)} custom-call(f32[384,128]{1,0:T(8,128)S(1)} %bitcast.10), custom_call_target="tpu_custom_call" | custom-call | tf_op jit(solution)/shard_map/unpack/pallas_call | solution.py:459
Async XLA Ops:
  0.6 13.5 %copy-start.1 = (bf16[384,384]{1,0:T(8,128)(2,1)S(1)}, bf16[384,384]{1,0:T(8,128)(2,1)}, u32[]{:S(2)}) copy-start(bf16[384,384]{1,0:T(8,128)(2,1)} %w_first_hbm.1) | copy-start | bytes 884740
  2.6 11.5 %copy-start.2 = (s32[512,127]{1,0:T(8,128)S(1)}, s32[512,127]{1,0:T(8,128)}, u32[]{:S(2)}) copy-start(s32[512,127]{1,0:T(8,128)} %flips_hbm.1) | copy-start | bytes 780292
  2.6 11.6 %copy-start.3 = (f32[3,1024]{1,0:T(4,128)S(1)}, f32[3,1024]{1,0:T(4,128)}, u32[]{:S(2)}) copy-start(f32[3,1024]{1,0:T(4,128)} %target_hbm.1) | copy-start | bytes 36868
  2.6 11.6 %copy-start.4 = (f32[384]{0:T(512)S(1)}, f32[384]{0:T(512)}, u32[]{:S(2)}) copy-start(f32[384]{0:T(512)} %b_first_hbm.1) | copy-start | bytes 4612
  2.6 11.6 %copy-start.5 = (bf16[384]{0:T(512)(128)(2,1)S(1)}, bf16[384]{0:T(512)(128)(2,1)}, u32[]{:S(2)}) copy-start(bf16[384]{0:T(512)(128)(2,1)} %w_second_hbm.1) | copy-start | bytes 2308
  2.6 11.6 %copy-start.6 = (bf16[127,128]{1,0:T(8,128)(2,1)S(1)}, bf16[127,128]{1,0:T(8,128)(2,1)}, u32[]{:S(2)}) copy-start(bf16[127,128]{1,0:T(8,128)(2,1)} %constant.2.clone.turns_hbm) | copy-start | bytes 97540
  2.7 22.1 %all-to-all-start = ((f32[128,1,384]{2,1,0:T(1,128)}), f32[128,1,384]{2,1,0:T(1,128)S(1)}, u32[]{:S(2)}, u32[]{:S(2)}) async-start(f32[128,1,384]{2,1,0:T(1,128)} %bitcast.13), calls=%async_computation | async-start | bytes 393216 | tf_op jit(solution)/shard_map/all_to_all | solution.py:404
  14.2 1.1 %copy-start = (bf16[1024,384]{1,0:T(8,128)(2,1)S(1)}, bf16[1024,384]{1,0:T(8,128)(2,1)}, u32[]{:S(2)}) copy-start(bf16[1024,384]{1,0:T(8,128)(2,1)} %feat_hbm.1) | copy-start | bytes 2359300

commit v4 on v3

--- a/solution.py
+++ b/solution.py
@@ -62,47 +62,33 @@
 
 
 def pixel_kernel(
-    w_first_hbm, b_first_hbm, w_second_hbm, feat_hbm, target_hbm, flips_hbm, turns_hbm,
-    pix_ref, before_ref, behind_ref,
-    w_first_ref, b_first_ref, w_second_ref, feat_ref, target_ref, flips_ref, turns_ref, arrived,
+    feat_ref, w_first_ref, b_first_ref, w_second_ref, target_ref, flips_hbm, turns_ref,
+    pix_ref, before_ref, behind_ref, flipped, arrived,
 ):
     me = lax.axis_index("region")
     first_row = pl.multiple_of(8 * (me // 2), 8)
-    pairs = [
-        (w_first_hbm, w_first_ref),
-        (b_first_hbm, b_first_ref),
-        (w_second_hbm, w_second_ref),
-        (target_hbm, target_ref),
-        (flips_hbm.at[pl.ds(first_row, 8), :], flips_ref),
-        (turns_hbm, turns_ref),
-    ] + [(feat_hbm.at[pl.ds(t * PIX, PIX), :], feat_ref.at[pl.ds(t * PIX, PIX), :]) for t in range(4)]
-    fetches = [
-        pltpu.make_async_copy(source, landing, arrived.at[n])
-        for n, (source, landing) in enumerate(pairs)
-    ]
-    for fetch in fetches:
-        fetch.start()
-    for fetch in fetches[:6]:
-        fetch.wait()
-    rows = jnp.broadcast_to(w_second_ref[...][None, :], (LANES, w_second_ref.shape[0]))
+    fetch = pltpu.make_async_copy(flips_hbm.at[pl.ds(first_row, 8), :], flipped, arrived)
+    fetch.start()
+    rows = jnp.broadcast_to(w_second_ref[...][None, :], (16, w_second_ref.shape[0]))
+    filler = jnp.zeros((LANES - 8, PIX), F32)
+    row = lax.broadcasted_iota(jnp.int32, (8, PIX), 0)
     bias = b_first_ref[...][None, :]
-    lane = lax.broadcasted_iota(jnp.int32, (PIX, LANES), 1)
-    filler = jnp.zeros((LANES - 3, PIX), F32)
     for t in range(4):
-        fetches[6 + t].wait()
         at = pl.ds(t * PIX, PIX)
         pre = jnp.dot(feat_ref[at, :], w_first_ref[...], preferred_element_type=F32) + bias
         hidden = jax.nn.gelu(pre).astype(BF16)
         score = lax.dot_general(
-            hidden, rows, (((1,), (1,)), ((), ())), preferred_element_type=F32
-        )
+            rows, hidden, (((1,), (1,)), ((), ())), preferred_element_type=F32
+        )[:8]
         spread = 0.5 + (jnp.maximum(score, 0.0) + jnp.log1p(jnp.exp(-jnp.abs(score))))
-        wanted = jnp.concatenate([target_ref[:, t * PIX : (t + 1) * PIX], filler], 0).T
-        pix_ref[at, :] = jnp.where(
-            lane == 3, 1.0 / (spread * spread), jnp.where(lane == 4, jnp.log(spread), wanted)
-        )
+        rest = jnp.where(row == 3, 1.0 / (spread * spread), jnp.log(spread))
+        wanted = target_ref[:, t * PIX : (t + 1) * PIX]
+        for c in range(3):
+            rest = jnp.where(row == c, wanted[c : c + 1], rest)
+        pix_ref[at, :] = jnp.concatenate([rest, filler], 0).T
+    fetch.wait()
     turned = jnp.dot(
-        flips_ref[...].astype(F32).astype(BF16), turns_ref[...], preferred_element_type=F32
+        flipped[...].astype(F32).astype(BF16), turns_ref[...], preferred_element_type=F32
     )
     ranks = jnp.where(me % 2 == 0, turned[:4], turned[4:])
     ranks = ranks + lax.broadcasted_iota(jnp.int32, (4, LANES), 1).astype(F32)
@@ -121,13 +107,14 @@
     )
 
 
-ROWS = 4
-STEPS = TSIDE // ROWS
+RENDER_ROWS = 4
+PULL_ROWS = 4
 
 
 def splat_kernel(
-    msg_ref, pix_ref, before_ref, behind_ref, loss_ref, out_ref,
+    msg_ref, pix_ref, before_ref, behind_ref, loss_hbm, out_ref,
     turned, places, sources, rows, across, alphas, weights, clear, color, carry, sums, grads,
+    loss_ref, sent,
 ):
     last_part = msg_ref[pl.ds(2, LANES, stride=3), :]
     turned[pl.ds(2 * LANES, LANES), :] = last_part.T
@@ -159,31 +146,33 @@
 
     fits = [counts[2 * s] + counts[2 * s + 1] <= LANES for s in range(2)]
 
-    def unit_y(s, k, step, r):
-        at = (step * ROWS + r).astype(F32) + 0.5
-        return (at - rows[s, k * 9 + 1]) * rows[s, k * 9 + 3]
+    turns = jnp.where(jnp.logical_and(fits[0], fits[1]), 1, 2)
+    send = pltpu.make_async_copy(loss_ref, loss_hbm, sent)
+
+    def unit_y(s, k, row):
+        return (row.astype(F32) + 0.5 - rows[s, k * 9 + 1]) * rows[s, k * 9 + 3]
 
     def render(step, unused):
         for s in range(2):
-            trans = [[None] * 2 for _ in range(ROWS)]
-            total = [[[None] * 3 for _ in range(2)] for _ in range(ROWS)]
+            trans = [[None] * 2 for _ in range(RENDER_ROWS)]
+            total = [[[None] * 3 for _ in range(2)] for _ in range(RENDER_ROWS)]
             for k in range(SPLATS):
                 shade = [rows[s, k * 9 + 6 + c] for c in range(3)]
-                for r in range(ROWS):
-                    down = unit_y(s, k, step, r)
+                for r in range(RENDER_ROWS):
+                    down = unit_y(s, k, step * RENDER_ROWS + r)
                     for h in range(2):
                         power = down * (across[s, k, h, 1] - down) - across[s, k, h, 2]
                         alpha = jnp.exp2(power)
                         weight = alpha if k == 0 else trans[r][h] * alpha
                         trans[r][h] = 1.0 - alpha if k == 0 else trans[r][h] - weight
-                        alphas[s, step, k, 2 * r + h] = alpha
-                        weights[s, step, k, 2 * r + h] = weight
+                        alphas[s, k, 2 * (step * RENDER_ROWS + r) + h] = alpha
+                        weights[s, k, 2 * (step * RENDER_ROWS + r) + h] = weight
                         for c in range(3):
                             term = weight * shade[c]
                             total[r][h][c] = term if k == 0 else total[r][h][c] + term
-            for r in range(ROWS):
+            for r in range(RENDER_ROWS):
                 for h in range(2):
-                    at = pl.ds(pl.multiple_of((step * ROWS + r) * 16 + 8 * h, 8), 8)
+                    at = pl.ds(pl.multiple_of((step * RENDER_ROWS + r) * 16 + 8 * h, 8), 8)
                     clear[s, at, :] = trans[r][h]
                     for c in range(3):
                         color[s, c, at, :] = total[r][h][c]
@@ -191,10 +180,10 @@
 
     def pull(step, unused):
         for s in range(2):
-            behind = [None] * (2 * ROWS)
-            slope = [[None] * 3 for _ in range(2 * ROWS)]
-            for n in range(2 * ROWS):
-                at = pl.ds(pl.multiple_of(step * (ROWS * 16) + 8 * n, 8), 8)
+            behind = [None] * (2 * PULL_ROWS)
+            slope = [[None] * 3 for _ in range(2 * PULL_ROWS)]
+            for n in range(2 * PULL_ROWS):
+                at = pl.ds(pl.multiple_of(step * (PULL_ROWS * 16) + 8 * n, 8), 8)
                 behind[n] = carry[s, at, :]
                 slope[n] = [color[s, c, at, :] for c in range(3)]
             for k in range(SPLATS - 1, -1, -1):
@@ -204,12 +193,12 @@
                 def add(n, value):
                     acc[n] = value if acc[n] is None else acc[n] + value
 
-                for r in range(ROWS):
-                    down = unit_y(s, k, step, r)
+                for r in range(PULL_ROWS):
+                    down = unit_y(s, k, step * PULL_ROWS + r)
                     for h in range(2):
                         n = 2 * r + h
-                        alpha = alphas[s, step, k, n]
-                        weight = weights[s, step, k, n]
+                        alpha = alphas[s, k, 2 * PULL_ROWS * step + n]
+                        weight = weights[s, k, 2 * PULL_ROWS * step + n]
                         gain = slope[n][0] * shade[0] + slope[n][1] * shade[1] + slope[n][2] * shade[2]
                         change = gain - behind[n]
                         behind[n] = behind[n] + alpha * change
@@ -365,18 +354,23 @@
         held = [constants(s, *flags[s]) for s in range(2)]
         for s in range(2):
             prepare(s, held[s][0], held[s][-1])
-        lax.fori_loop(0, STEPS, render, 0)
+        lax.fori_loop(0, TSIDE // RENDER_ROWS, render, 0)
         composite(flags)
+
+        @pl.when(turn == turns - 1)
+        def _():
+            send.start()
+
         sums[...] = jnp.zeros_like(sums)
-        lax.fori_loop(0, STEPS, pull, 0)
+        lax.fori_loop(0, TSIDE // PULL_ROWS, pull, 0)
         for s in range(2):
             finish(s, flags[s], *held[s][:-1])
         return 0
 
-    turns = jnp.where(jnp.logical_and(fits[0], fits[1]), 1, 2)
     lax.fori_loop(0, turns, both_blocks, 0)
     for b in range(3):
         out_ref[pl.ds(b, LANES, stride=3), :] = grads[pl.ds(b * LANES, LANES), :].T
+    send.wait()
 
 
 def order_matrix(regions):
@@ -414,25 +408,26 @@
     received = exchange(message)
 
     order = jax.ShapeDtypeStruct((4, LANES, LANES), BF16)
-    operands = (
-        w_first, b_first, w_second, features, target, flips, jnp.asarray(order_matrix(regions), BF16)
-    )
-    landings = [pltpu.VMEM(x.shape, x.dtype) for x in operands]
-    landings[5] = pltpu.VMEM((8, regions - 1), jnp.int32)
     pix, before, behind = pl.pallas_call(
         pixel_kernel,
-        in_specs=[pl.BlockSpec(memory_space=pltpu.HBM)] * 7,
+        in_specs=[pl.BlockSpec(memory_space=pltpu.VMEM)] * 5
+        + [pl.BlockSpec(memory_space=pl.ANY), pl.BlockSpec(memory_space=pltpu.VMEM)],
         out_shape=(jax.ShapeDtypeStruct((4 * PIX, LANES), F32), order, order),
-        scratch_shapes=landings + [pltpu.SemaphoreType.DMA((10,))],
+        scratch_shapes=[vmem(8, regions - 1, dtype=jnp.int32), pltpu.SemaphoreType.DMA],
         compiler_params=limit,
         cost_estimate=pl.CostEstimate(
             flops=2 * 1024 * 384 * 512, bytes_accessed=2_000_000, transcendentals=1024 * 384
         ),
         name="pixels",
-    )(*operands)
+    )(
+        features, w_first, b_first, w_second, target, flips,
+        jnp.asarray(order_matrix(regions), BF16),
+    )
 
     loss, returned = pl.pallas_call(
         splat_kernel,
+        in_specs=[pl.BlockSpec(memory_space=pltpu.VMEM)] * 4,
+        out_specs=(pl.BlockSpec(memory_space=pl.ANY), pl.BlockSpec(memory_space=pltpu.VMEM)),
         out_shape=(
             jax.ShapeDtypeStruct((8, LANES), F32),
             jax.ShapeDtypeStruct((3 * regions, LANES), F32),
@@ -443,13 +438,15 @@
             vmem(4, 8, LANES, dtype=jnp.int32),
             vmem(2, 72, 8, LANES),
             vmem(2, SPLATS, 2, 3, 8, LANES),
-            vmem(2, STEPS, SPLATS, 2 * ROWS, 8, LANES),
-            vmem(2, STEPS, SPLATS, 2 * ROWS, 8, LANES),
+            vmem(2, SPLATS, PIX // 8, 8, LANES),
+            vmem(2, SPLATS, PIX // 8, 8, LANES),
             vmem(2, PIX, LANES),
             vmem(2, 3, PIX, LANES),
             vmem(2, PIX, LANES),
             vmem(2, 72, 8, LANES),
             vmem(WIDTH, LANES),
+            vmem(8, LANES),
+            pltpu.SemaphoreType.DMA,
         ],
         compiler_params=limit,
         name="splats",

time: 45 us -> 44.8 us (level)
  Pallas kernels: 10.9 us -> 9.05 us
  waiting for transfers between devices: 5.96 us -> 7.6 us
    pallas_call x2, Pallas kernels: 8.06 us -> 6.22 us  [the longest x1 4.48 us: shards(): pl.pallas_call(splat_kernel, in_specs=[pl.BlockSpec(memory_space=pltpu.VM...]
    all_to_all x1, waiting for transfers between devices: 5.96 us -> 7.6 us  [exchange(): lax.all_to_all(rows.reshape(regions, 1, WIDTH), 'region', 0, 0, tiled=True)]
  transfers between devices with their start and end apart: 1 -> 1, of which waited for: 1 -> 1; matrix products, arithmetic and copies ran while one was open for 0% -> 0% of each run, Pallas kernels for 8% -> 4%
where the time goes in v4:
time: 44.8 us; the launch traced here: 44.6 us
  blocking collectives  14.5 us (32%)
  starting transfers between devices  11.5 us (26%)
  Pallas kernels  9.05 us (20%)
  waiting for transfers between devices  7.6 us (17%)
  local copies, waits for them, and re-layouts  1.15 us (3%)
  between operations  0.73 us (2%)
    all_to_all x1, blocking collectives, exchange(): lax.all_to_all(rows.reshape(regions, 1, WIDTH), 'region', 0, 0, tiled=True)  14.5 us
    all_to_all x1, starting transfers between devices, exchange(): lax.all_to_all(rows.reshape(regions, 1, WIDTH), 'region', 0, 0, tiled=True)  11.5 us
    all_to_all x1, waiting for transfers between devices, exchange(): lax.all_to_all(rows.reshape(regions, 1, WIDTH), 'region', 0, 0, tiled=True)  7.6 us
    pallas_call x1, Pallas kernels, shards(): pl.pallas_call(splat_kernel, in_specs=[pl.BlockSpec(memory_space=pltpu.VM...  4.48 us
    pallas_call x1, Pallas kernels, shards(): pl.pallas_call(pack_kernel, out_shape=jax.ShapeDtypeStruct((3 * regions,...  1.99 us
    pallas_call x1, Pallas kernels, shards(): pl.pallas_call(pixel_kernel, in_specs=[pl.BlockSpec(memory_space=pltpu.VM...  1.74 us
    unnamed x14, local copies, waits for them, and re-layouts  1.15 us
  transfers between devices with their start and end apart: 1, of which 1 were waited for; matrix products, arithmetic and copies ran while one was open for 0% of the time, Pallas kernels for 4%

profile of v4, /device:TPU:1, one launch (start us, length us, event | category | flops | bytes accessed | tf_op | source)
XLA Modules:
  0.0 44.6 jit_solution(4232574208180587938)
XLA Ops:
  0.6 0.0 copy-start.1
  0.6 2.0 %pack.1 = f32[384,128]{1,0:T(8,128)} custom-call(f32[9,32,128]{2,1,0:T(8,128)} %bitcast.14, s32[8,512]{1,0:T(8,128)} %bitcast.16, s32[1,512]{1,0:T(1,128)} %cover_ref.1), custom_call_target="tpu_custom_call" | custom-call | tf_op jit(solution)/shard_map/pack/pallas_call | solution.py:401
  2.6 0.0 copy-start.2
  2.6 0.0 copy-start.3
  2.6 0.0 copy-start.4
  2.6 0.0 copy-start.5
  2.6 0.0 copy-start.6
  2.7 11.5 %all-to-all-start = ((f32[128,1,384]{2,1,0:T(1,128)}), f32[128,1,384]{2,1,0:T(1,128)S(1)}, u32[]{:S(2)}, u32[]{:S(2)}) async-start(f32[128,1,384]{2,1,0:T(1,128)} %bitcast.13), calls=%async_computation | async-start | bytes 393216 | tf_op jit(solution)/shard_map/all_to_all | solution.py:398
  14.2 0.0 copy-done.1
  14.2 0.0 copy-done.2
  14.2 0.0 copy-done.3
  14.2 0.0 copy-done.4
  14.2 0.0 copy-done.5
  14.2 0.0 copy-done.6
  14.2 0.0 copy-start
  14.2 1.1 %copy-done = bf16[1024,384]{1,0:T(8,128)(2,1)S(1)} copy-done((bf16[1024,384]{1,0:T(8,128)(2,1)S(1)}, bf16[1024,384]{1,0:T(8,128)(2,1)}, u32[]{:S(2)}) %copy-start) | copy-done | bytes 786456
  15.4 1.7 %pixels.1 = (f32[1024,128]{1,0:T(8,128)S(1)}, bf16[4,128,128]{2,1,0:T(8,128)(2,1)S(1)}, bf16[4,128,128]{2,1,0:T(8,128)(2,1)S(1)}) custom-call(bf16[1024,384]{1,0:T(8,128)(2,1)S(1)} %copy-done, bf16[384,384]{1,0:T(8,128)(2,1)S(1)} %copy-done.1, f32[384]{0:T(512)S(1)} %copy-done.4, bf16[384]{0:T(512)(128)(2,1)S(1)} %copy-done.5, f32[3,1024]{1,0:T(4,128)S(1)} %copy-done.3, ...), custom_call_target="tpu_custom_call" | custom-call | flops 402653184 | bytes 2000000 | tf_op jit(solution)/shard_map/pixels/pallas_call | solution.py:411
  17.1 7.6 %all-to-all-done = f32[128,1,384]{2,1,0:T(1,128)S(1)} async-done(((f32[128,1,384]{2,1,0:T(1,128)}), f32[128,1,384]{2,1,0:T(1,128)S(1)}, u32[]{:S(2)}, u32[]{:S(2)}) %all-to-all-start) | async-done | bytes 196640 | tf_op jit(solution)/shard_map/all_to_all | solution.py:398
  24.7 4.5 %splats.1 = (f32[8,128]{1,0:T(8,128)}, f32[384,128]{1,0:T(8,128)S(1)}) custom-call(f32[384,128]{1,0:T(8,128)S(1)} %bitcast.11, f32[1024,128]{1,0:T(8,128)S(1)} %get-tuple-element.7.pix_ref, bf16[4,128,128]{2,1,0:T(8,128)(2,1)S(1)} %get-tuple-element.8.before_ref, bf16[4,128,128]{2,1,0:T(8,128)(2,1)S(1)} %get-tuple-element.9.behind_ref), custom_call_target="tpu_custom_call" | custom-call | tf_op jit(solution)/shard_map/splats/pallas_call | solution.py:427
  29.2 14.5 %all_to_all.10 = f32[128,1,384]{2,1,0:T(1,128)S(1)} all-to-all(f32[128,1,384]{2,1,0:T(1,128)S(1)} %bitcast.12), channel_id=1, replica_groups=mesh['region'=128] {'region'}, dimensions={0} | all-to-all | bytes 393216 | tf_op jit(solution)/shard_map/all_to_all | solution.py:398
  43.7 0.8 %unpack.1 = f32[9,32,128]{2,1,0:T(8,128)} custom-call(f32[384,128]{1,0:T(8,128)S(1)} %bitcast.10), custom_call_target="tpu_custom_call" | custom-call | tf_op jit(solution)/shard_map/unpack/pallas_call | solution.py:456
Async XLA Ops:
  0.6 13.5 %copy-start.1 = (bf16[384,384]{1,0:T(8,128)(2,1)S(1)}, bf16[384,384]{1,0:T(8,128)(2,1)}, u32[]{:S(2)}) copy-start(bf16[384,384]{1,0:T(8,128)(2,1)} %w_first_ref.1) | copy-start | bytes 884740
  2.6 11.5 %copy-start.2 = (s32[512,127]{1,0:T(8,128)S(1)}, s32[512,127]{1,0:T(8,128)}, u32[]{:S(2)}) copy-start(s32[512,127]{1,0:T(8,128)} %flips_hbm.1) | copy-start | bytes 780292
  2.6 11.6 %copy-start.3 = (f32[3,1024]{1,0:T(4,128)S(1)}, f32[3,1024]{1,0:T(4,128)}, u32[]{:S(2)}) copy-start(f32[3,1024]{1,0:T(4,128)} %target_ref.1) | copy-start | bytes 36868
  2.6 11.6 %copy-start.4 = (f32[384]{0:T(512)S(1)}, f32[384]{0:T(512)}, u32[]{:S(2)}) copy-start(f32[384]{0:T(512)} %b_first_ref.1) | copy-start | bytes 4612
  2.6 11.6 %copy-start.5 = (bf16[384]{0:T(512)(128)(2,1)S(1)}, bf16[384]{0:T(512)(128)(2,1)}, u32[]{:S(2)}) copy-start(bf16[384]{0:T(512)(128)(2,1)} %w_second_ref.1) | copy-start | bytes 2308
  2.6 11.6 %copy-start.6 = (bf16[127,128]{1,0:T(8,128)(2,1)S(1)}, bf16[127,128]{1,0:T(8,128)(2,1)}, u32[]{:S(2)}) copy-start(bf16[127,128]{1,0:T(8,128)(2,1)} %constant.2.clone.turns_ref) | copy-start | bytes 97540
  2.7 22.1 %all-to-all-start = ((f32[128,1,384]{2,1,0:T(1,128)}), f32[128,1,384]{2,1,0:T(1,128)S(1)}, u32[]{:S(2)}, u32[]{:S(2)}) async-start(f32[128,1,384]{2,1,0:T(1,128)} %bitcast.13), calls=%async_computation | async-start | bytes 393216 | tf_op jit(solution)/shard_map/all_to_all | solution.py:398
  14.2 1.1 %copy-start = (bf16[1024,384]{1,0:T(8,128)(2,1)S(1)}, bf16[1024,384]{1,0:T(8,128)(2,1)}, u32[]{:S(2)}) copy-start(bf16[1024,384]{1,0:T(8,128)(2,1)} %feat_ref.1) | copy-start | bytes 2359300

commit v5 on v4

--- a/solution.py
+++ b/solution.py
@@ -113,7 +113,7 @@
 
 def splat_kernel(
     msg_ref, pix_ref, before_ref, behind_ref, loss_hbm, out_ref,
-    turned, places, sources, rows, across, alphas, weights, clear, color, carry, sums, grads,
+    turned, places, sources, rows, across, downs, alphas, weights, clear, color, carry, sums, grads,
     loss_ref, sent,
 ):
     last_part = msg_ref[pl.ds(2, LANES, stride=3), :]
@@ -160,6 +160,7 @@
                 shade = [rows[s, k * 9 + 6 + c] for c in range(3)]
                 for r in range(RENDER_ROWS):
                     down = unit_y(s, k, step * RENDER_ROWS + r)
+                    downs[s, k, step * RENDER_ROWS + r] = down
                     for h in range(2):
                         power = down * (across[s, k, h, 1] - down) - across[s, k, h, 2]
                         alpha = jnp.exp2(power)
@@ -188,13 +189,14 @@
                 slope[n] = [color[s, c, at, :] for c in range(3)]
             for k in range(SPLATS - 1, -1, -1):
                 shade = [rows[s, k * 9 + 6 + c] for c in range(3)]
-                acc = [None] * 9
+                acc = [None] * 8
 
                 def add(n, value):
                     acc[n] = value if acc[n] is None else acc[n] + value
 
                 for r in range(PULL_ROWS):
-                    down = unit_y(s, k, step * PULL_ROWS + r)
+                    down = downs[s, k, step * PULL_ROWS + r]
+                    both = None
                     for h in range(2):
                         n = 2 * r + h
                         alpha = alphas[s, k, 2 * PULL_ROWS * step + n]
@@ -204,13 +206,14 @@
                         behind[n] = behind[n] + alpha * change
                         pulled = weight * change
                         leaned = pulled * down
-                        add(3 * h, pulled)
-                        add(3 * h + 1, leaned)
-                        add(3 * h + 2, leaned * down)
+                        both = leaned if h == 0 else both + leaned
+                        add(2 * h, pulled)
+                        add(2 * h + 1, leaned)
                         for c in range(3):
-                            add(6 + c, weight * slope[n][c])
-                for n in range(9):
-                    sums[s, k * 9 + n] = sums[s, k * 9 + n] + acc[n]
+                            add(5 + c, weight * slope[n][c])
+                    add(4, both * down)
+                for n in range(8):
+                    sums[s, k * 8 + n] = sums[s, k * 8 + n] + acc[n]
         return 0
 
     def constants(s, has_first, has_last):
@@ -308,7 +311,7 @@
         plain_sums = [None] * 9
         for k in range(SPLATS):
             chosen = ranks == float(k)
-            left, right = [[sums[s, k * 9 + 3 * h + n] for n in range(3)] for h in range(2)]
+            left, right = [[sums[s, k * 8 + 2 * h + n] for n in range(2)] for h in range(2)]
             u0, u1 = across[s, k, 0, 0], across[s, k, 1, 0]
             m0, m1 = left[0] * u0, right[0] * u1
             moments = [
@@ -317,8 +320,8 @@
                 left[1] + right[1],
                 m0 * u0 + m1 * u1,
                 left[1] * u0 + right[1] * u1,
-                left[2] + right[2],
-            ] + [sums[s, k * 9 + 6 + c] for c in range(3)]
+                sums[s, k * 8 + 4],
+            ] + [sums[s, k * 8 + 5 + c] for c in range(3)]
             for n, value in enumerate(moments):
                 row = jnp.broadcast_to(jnp.sum(value, axis=0, keepdims=True), (8, LANES))
                 plain_sums[n] = (
@@ -438,12 +441,13 @@
             vmem(4, 8, LANES, dtype=jnp.int32),
             vmem(2, 72, 8, LANES),
             vmem(2, SPLATS, 2, 3, 8, LANES),
+            vmem(2, SPLATS, TSIDE, 8, LANES),
             vmem(2, SPLATS, PIX // 8, 8, LANES),
             vmem(2, SPLATS, PIX // 8, 8, LANES),
             vmem(2, PIX, LANES),
             vmem(2, 3, PIX, LANES),
             vmem(2, PIX, LANES),
-            vmem(2, 72, 8, LANES),
+            vmem(2, 64, 8, LANES),
             vmem(WIDTH, LANES),
             vmem(8, LANES),
             pltpu.SemaphoreType.DMA,

time: 44.8 us -> 44.7 us (level)
  no operation moved by 1% of the time
where the time goes in v5:
time: 44.7 us; the launch traced here: 44.5 us
  blocking collectives  14.5 us (32%)
  starting transfers between devices  11.5 us (26%)
  Pallas kernels  8.95 us (20%)
  waiting for transfers between devices  7.6 us (17%)
  local copies, waits for them, and re-layouts  1.15 us (3%)
  between operations  0.73 us (2%)
    all_to_all x1, blocking collectives, exchange(): lax.all_to_all(rows.reshape(regions, 1, WIDTH), 'region', 0, 0, tiled=True)  14.5 us
    all_to_all x1, starting transfers between devices, exchange(): lax.all_to_all(rows.reshape(regions, 1, WIDTH), 'region', 0, 0, tiled=True)  11.5 us
    all_to_all x1, waiting for transfers between devices, exchange(): lax.all_to_all(rows.reshape(regions, 1, WIDTH), 'region', 0, 0, tiled=True)  7.6 us
    pallas_call x1, Pallas kernels, shards(): pl.pallas_call(splat_kernel, in_specs=[pl.BlockSpec(memory_space=pltpu.VM...  4.39 us
    pallas_call x1, Pallas kernels, shards(): pl.pallas_call(pack_kernel, out_shape=jax.ShapeDtypeStruct((3 * regions,...  1.99 us
    pallas_call x1, Pallas kernels, shards(): pl.pallas_call(pixel_kernel, in_specs=[pl.BlockSpec(memory_space=pltpu.VM...  1.74 us
    unnamed x14, local copies, waits for them, and re-layouts  1.15 us
  transfers between devices with their start and end apart: 1, of which 1 were waited for; matrix products, arithmetic and copies ran while one was open for 0% of the time, Pallas kernels for 4%

profile of v5, /device:TPU:1, one launch (start us, length us, event | category | flops | bytes accessed | tf_op | source)
XLA Modules:
  0.0 44.5 jit_solution(5670434519639736017)
XLA Ops:
  0.6 0.0 copy-start.1
  0.6 2.0 %pack.1 = f32[384,128]{1,0:T(8,128)} custom-call(f32[9,32,128]{2,1,0:T(8,128)} %bitcast.14, s32[8,512]{1,0:T(8,128)} %bitcast.16, s32[1,512]{1,0:T(1,128)} %cover_ref.1), custom_call_target="tpu_custom_call" | custom-call | tf_op jit(solution)/shard_map/pack/pallas_call | solution.py:404
  2.6 0.0 copy-start.2
  2.6 0.0 copy-start.3
  2.6 0.0 copy-start.4
  2.6 0.0 copy-start.5
  2.6 0.0 copy-start.6
  2.7 11.5 %all-to-all-start = ((f32[128,1,384]{2,1,0:T(1,128)}), f32[128,1,384]{2,1,0:T(1,128)S(1)}, u32[]{:S(2)}, u32[]{:S(2)}) async-start(f32[128,1,384]{2,1,0:T(1,128)} %bitcast.13), calls=%async_computation | async-start | bytes 393216 | tf_op jit(solution)/shard_map/all_to_all | solution.py:401
  14.2 0.0 copy-done.1
  14.2 0.0 copy-done.2
  14.2 0.0 copy-done.3
  14.2 0.0 copy-done.4
  14.2 0.0 copy-done.5
  14.2 0.0 copy-done.6
  14.2 0.0 copy-start
  14.2 1.1 %copy-done = bf16[1024,384]{1,0:T(8,128)(2,1)S(1)} copy-done((bf16[1024,384]{1,0:T(8,128)(2,1)S(1)}, bf16[1024,384]{1,0:T(8,128)(2,1)}, u32[]{:S(2)}) %copy-start) | copy-done | bytes 786456
  15.4 1.7 %pixels.1 = (f32[1024,128]{1,0:T(8,128)S(1)}, bf16[4,128,128]{2,1,0:T(8,128)(2,1)S(1)}, bf16[4,128,128]{2,1,0:T(8,128)(2,1)S(1)}) custom-call(bf16[1024,384]{1,0:T(8,128)(2,1)S(1)} %copy-done, bf16[384,384]{1,0:T(8,128)(2,1)S(1)} %copy-done.1, f32[384]{0:T(512)S(1)} %copy-done.4, bf16[384]{0:T(512)(128)(2,1)S(1)} %copy-done.5, f32[3,1024]{1,0:T(4,128)S(1)} %copy-done.3, ...), custom_call_target="tpu_custom_call" | custom-call | flops 402653184 | bytes 2000000 | tf_op jit(solution)/shard_map/pixels/pallas_call | solution.py:414
  17.1 7.6 %all-to-all-done = f32[128,1,384]{2,1,0:T(1,128)S(1)} async-done(((f32[128,1,384]{2,1,0:T(1,128)}), f32[128,1,384]{2,1,0:T(1,128)S(1)}, u32[]{:S(2)}, u32[]{:S(2)}) %all-to-all-start) | async-done | bytes 196640 | tf_op jit(solution)/shard_map/all_to_all | solution.py:401
  24.7 4.4 %splats.1 = (f32[8,128]{1,0:T(8,128)}, f32[384,128]{1,0:T(8,128)S(1)}) custom-call(f32[384,128]{1,0:T(8,128)S(1)} %bitcast.11, f32[1024,128]{1,0:T(8,128)S(1)} %get-tuple-element.7.pix_ref, bf16[4,128,128]{2,1,0:T(8,128)(2,1)S(1)} %get-tuple-element.8.before_ref, bf16[4,128,128]{2,1,0:T(8,128)(2,1)S(1)} %get-tuple-element.9.behind_ref), custom_call_target="tpu_custom_call" | custom-call | tf_op jit(solution)/shard_map/splats/pallas_call | solution.py:430
  29.1 14.5 %all_to_all.10 = f32[128,1,384]{2,1,0:T(1,128)S(1)} all-to-all(f32[128,1,384]{2,1,0:T(1,128)S(1)} %bitcast.12), channel_id=1, replica_groups=mesh['region'=128] {'region'}, dimensions={0} | all-to-all | bytes 393216 | tf_op jit(solution)/shard_map/all_to_all | solution.py:401
  43.6 0.8 %unpack.1 = f32[9,32,128]{2,1,0:T(8,128)} custom-call(f32[384,128]{1,0:T(8,128)S(1)} %bitcast.10), custom_call_target="tpu_custom_call" | custom-call | tf_op jit(solution)/shard_map/unpack/pallas_call | solution.py:460
Async XLA Ops:
  0.6 13.5 %copy-start.1 = (bf16[384,384]{1,0:T(8,128)(2,1)S(1)}, bf16[384,384]{1,0:T(8,128)(2,1)}, u32[]{:S(2)}) copy-start(bf16[384,384]{1,0:T(8,128)(2,1)} %w_first_ref.1) | copy-start | bytes 884740
  2.6 11.5 %copy-start.2 = (s32[512,127]{1,0:T(8,128)S(1)}, s32[512,127]{1,0:T(8,128)}, u32[]{:S(2)}) copy-start(s32[512,127]{1,0:T(8,128)} %flips_hbm.1) | copy-start | bytes 780292
  2.6 11.6 %copy-start.3 = (f32[3,1024]{1,0:T(4,128)S(1)}, f32[3,1024]{1,0:T(4,128)}, u32[]{:S(2)}) copy-start(f32[3,1024]{1,0:T(4,128)} %target_ref.1) | copy-start | bytes 36868
  2.6 11.6 %copy-start.4 = (f32[384]{0:T(512)S(1)}, f32[384]{0:T(512)}, u32[]{:S(2)}) copy-start(f32[384]{0:T(512)} %b_first_ref.1) | copy-start | bytes 4612
  2.6 11.6 %copy-start.5 = (bf16[384]{0:T(512)(128)(2,1)S(1)}, bf16[384]{0:T(512)(128)(2,1)}, u32[]{:S(2)}) copy-start(bf16[384]{0:T(512)(128)(2,1)} %w_second_ref.1) | copy-start | bytes 2308
  2.6 11.6 %copy-start.6 = (bf16[127,128]{1,0:T(8,128)(2,1)S(1)}, bf16[127,128]{1,0:T(8,128)(2,1)}, u32[]{:S(2)}) copy-start(bf16[127,128]{1,0:T(8,128)(2,1)} %constant.2.clone.turns_ref) | copy-start | bytes 97540
  2.7 22.1 %all-to-all-start = ((f32[128,1,384]{2,1,0:T(1,128)}), f32[128,1,384]{2,1,0:T(1,128)S(1)}, u32[]{:S(2)}, u32[]{:S(2)}) async-start(f32[128,1,384]{2,1,0:T(1,128)} %bitcast.13), calls=%async_computation | async-start | bytes 393216 | tf_op jit(solution)/shard_map/all_to_all | solution.py:401
  14.2 1.1 %copy-start = (bf16[1024,384]{1,0:T(8,128)(2,1)S(1)}, bf16[1024,384]{1,0:T(8,128)(2,1)}, u32[]{:S(2)}) copy-start(bf16[1024,384]{1,0:T(8,128)(2,1)} %feat_ref.1) | copy-start | bytes 2359300

commit v6 on v5

--- a/solution.py
+++ b/solution.py
@@ -245,11 +245,14 @@
         return ranks, inv_x, inv_y, curl, rho, inv_det, scale, odds, tint, plain
 
     def prepare(s, ranks, plain):
+        order = jnp.zeros((8, LANES), F32)
+        for g in range(1, SPLATS):
+            order = jnp.where(ranks[g : g + 1] == sub, float(g), order)
+        order = order.astype(jnp.int32)
+        plain = [jnp.take_along_axis(value, order, axis=0) for value in plain]
         for k in range(SPLATS):
-            chosen = ranks == float(k)
             for n, value in enumerate(plain):
-                row = jnp.sum(jnp.where(chosen, value, 0.0), axis=0, keepdims=True)
-                rows[s, k * 9 + n] = jnp.broadcast_to(row, (8, LANES))
+                rows[s, k * 9 + n] = jnp.broadcast_to(value[k : k + 1], (8, LANES))
             for h in range(2):
                 unit = (sub + (0.5 + 8.0 * h) - rows[s, k * 9]) * rows[s, k * 9 + 2]
                 across[s, k, h, 0] = unit

time: 44.7 us -> 44.6 us (level)
  no operation moved by 1% of the time
where the time goes in v6:
time: 44.6 us; the launch traced here: 44.4 us
  blocking collectives  14.5 us (33%)
  starting transfers between devices  11.5 us (26%)
  Pallas kernels  8.85 us (20%)
  waiting for transfers between devices  7.6 us (17%)
  local copies, waits for them, and re-layouts  1.15 us (3%)
  between operations  0.73 us (2%)
    all_to_all x1, blocking collectives, exchange(): lax.all_to_all(rows.reshape(regions, 1, WIDTH), 'region', 0, 0, tiled=True)  14.5 us
    all_to_all x1, starting transfers between devices, exchange(): lax.all_to_all(rows.reshape(regions, 1, WIDTH), 'region', 0, 0, tiled=True)  11.5 us
    all_to_all x1, waiting for transfers between devices, exchange(): lax.all_to_all(rows.reshape(regions, 1, WIDTH), 'region', 0, 0, tiled=True)  7.6 us
    pallas_call x1, Pallas kernels, shards(): pl.pallas_call(splat_kernel, in_specs=[pl.BlockSpec(memory_space=pltpu.VM...  4.28 us
    pallas_call x1, Pallas kernels, shards(): pl.pallas_call(pack_kernel, out_shape=jax.ShapeDtypeStruct((3 * regions,...  1.99 us
    pallas_call x1, Pallas kernels, shards(): pl.pallas_call(pixel_kernel, in_specs=[pl.BlockSpec(memory_space=pltpu.VM...  1.74 us
    unnamed x14, local copies, waits for them, and re-layouts  1.15 us
  transfers between devices with their start and end apart: 1, of which 1 were waited for; matrix products, arithmetic and copies ran while one was open for 0% of the time, Pallas kernels for 4%

profile of v6, /device:TPU:1, one launch (start us, length us, event | category | flops | bytes accessed | tf_op | source)
XLA Modules:
  0.0 44.4 jit_solution(1613205627721310273)
XLA Ops:
  0.6 0.0 copy-start.1
  0.6 2.0 %pack.1 = f32[384,128]{1,0:T(8,128)} custom-call(f32[9,32,128]{2,1,0:T(8,128)} %bitcast.14, s32[8,512]{1,0:T(8,128)} %bitcast.16, s32[1,512]{1,0:T(1,128)} %cover_ref.1), custom_call_target="tpu_custom_call" | custom-call | tf_op jit(solution)/shard_map/pack/pallas_call | solution.py:407
  2.6 0.0 copy-start.2
  2.6 0.0 copy-start.3
  2.6 0.0 copy-start.4
  2.6 0.0 copy-start.5
  2.6 0.0 copy-start.6
  2.7 11.5 %all-to-all-start = ((f32[128,1,384]{2,1,0:T(1,128)}), f32[128,1,384]{2,1,0:T(1,128)S(1)}, u32[]{:S(2)}, u32[]{:S(2)}) async-start(f32[128,1,384]{2,1,0:T(1,128)} %bitcast.13), calls=%async_computation | async-start | bytes 393216 | tf_op jit(solution)/shard_map/all_to_all | solution.py:404
  14.2 0.0 copy-done.1
  14.2 0.0 copy-done.2
  14.2 0.0 copy-done.3
  14.2 0.0 copy-done.4
  14.2 0.0 copy-done.5
  14.2 0.0 copy-done.6
  14.2 0.0 copy-start
  14.2 1.1 %copy-done = bf16[1024,384]{1,0:T(8,128)(2,1)S(1)} copy-done((bf16[1024,384]{1,0:T(8,128)(2,1)S(1)}, bf16[1024,384]{1,0:T(8,128)(2,1)}, u32[]{:S(2)}) %copy-start) | copy-done | bytes 786456
  15.4 1.7 %pixels.1 = (f32[1024,128]{1,0:T(8,128)S(1)}, bf16[4,128,128]{2,1,0:T(8,128)(2,1)S(1)}, bf16[4,128,128]{2,1,0:T(8,128)(2,1)S(1)}) custom-call(bf16[1024,384]{1,0:T(8,128)(2,1)S(1)} %copy-done, bf16[384,384]{1,0:T(8,128)(2,1)S(1)} %copy-done.1, f32[384]{0:T(512)S(1)} %copy-done.4, bf16[384]{0:T(512)(128)(2,1)S(1)} %copy-done.5, f32[3,1024]{1,0:T(4,128)S(1)} %copy-done.3, ...), custom_call_target="tpu_custom_call" | custom-call | flops 402653184 | bytes 2000000 | tf_op jit(solution)/shard_map/pixels/pallas_call | solution.py:417
  17.1 7.6 %all-to-all-done = f32[128,1,384]{2,1,0:T(1,128)S(1)} async-done(((f32[128,1,384]{2,1,0:T(1,128)}), f32[128,1,384]{2,1,0:T(1,128)S(1)}, u32[]{:S(2)}, u32[]{:S(2)}) %all-to-all-start) | async-done | bytes 196640 | tf_op jit(solution)/shard_map/all_to_all | solution.py:404
  24.7 4.3 %splats.1 = (f32[8,128]{1,0:T(8,128)}, f32[384,128]{1,0:T(8,128)S(1)}) custom-call(f32[384,128]{1,0:T(8,128)S(1)} %bitcast.11, f32[1024,128]{1,0:T(8,128)S(1)} %get-tuple-element.7.pix_ref, bf16[4,128,128]{2,1,0:T(8,128)(2,1)S(1)} %get-tuple-element.8.before_ref, bf16[4,128,128]{2,1,0:T(8,128)(2,1)S(1)} %get-tuple-element.9.behind_ref), custom_call_target="tpu_custom_call" | custom-call | tf_op jit(solution)/shard_map/splats/pallas_call | solution.py:433
  29.0 14.5 %all_to_all.10 = f32[128,1,384]{2,1,0:T(1,128)S(1)} all-to-all(f32[128,1,384]{2,1,0:T(1,128)S(1)} %bitcast.12), channel_id=1, replica_groups=mesh['region'=128] {'region'}, dimensions={0} | all-to-all | bytes 393216 | tf_op jit(solution)/shard_map/all_to_all | solution.py:404
  43.5 0.8 %unpack.1 = f32[9,32,128]{2,1,0:T(8,128)} custom-call(f32[384,128]{1,0:T(8,128)S(1)} %bitcast.10), custom_call_target="tpu_custom_call" | custom-call | tf_op jit(solution)/shard_map/unpack/pallas_call | solution.py:463
Async XLA Ops:
  0.6 13.5 %copy-start.1 = (bf16[384,384]{1,0:T(8,128)(2,1)S(1)}, bf16[384,384]{1,0:T(8,128)(2,1)}, u32[]{:S(2)}) copy-start(bf16[384,384]{1,0:T(8,128)(2,1)} %w_first_ref.1) | copy-start | bytes 884740
  2.6 11.5 %copy-start.2 = (s32[512,127]{1,0:T(8,128)S(1)}, s32[512,127]{1,0:T(8,128)}, u32[]{:S(2)}) copy-start(s32[512,127]{1,0:T(8,128)} %flips_hbm.1) | copy-start | bytes 780292
  2.6 11.6 %copy-start.3 = (f32[3,1024]{1,0:T(4,128)S(1)}, f32[3,1024]{1,0:T(4,128)}, u32[]{:S(2)}) copy-start(f32[3,1024]{1,0:T(4,128)} %target_ref.1) | copy-start | bytes 36868
  2.6 11.6 %copy-start.4 = (f32[384]{0:T(512)S(1)}, f32[384]{0:T(512)}, u32[]{:S(2)}) copy-start(f32[384]{0:T(512)} %b_first_ref.1) | copy-start | bytes 4612
  2.6 11.6 %copy-start.5 = (bf16[384]{0:T(512)(128)(2,1)S(1)}, bf16[384]{0:T(512)(128)(2,1)}, u32[]{:S(2)}) copy-start(bf16[384]{0:T(512)(128)(2,1)} %w_second_ref.1) | copy-start | bytes 2308
  2.6 11.6 %copy-start.6 = (bf16[127,128]{1,0:T(8,128)(2,1)S(1)}, bf16[127,128]{1,0:T(8,128)(2,1)}, u32[]{:S(2)}) copy-start(bf16[127,128]{1,0:T(8,128)(2,1)} %constant.2.clone.turns_ref) | copy-start | bytes 97540
  2.7 22.1 %all-to-all-start = ((f32[128,1,384]{2,1,0:T(1,128)}), f32[128,1,384]{2,1,0:T(1,128)S(1)}, u32[]{:S(2)}, u32[]{:S(2)}) async-start(f32[128,1,384]{2,1,0:T(1,128)} %bitcast.13), calls=%async_computation | async-start | bytes 393216 | tf_op jit(solution)/shard_map/all_to_all | solution.py:404
  14.2 1.1 %copy-start = (bf16[1024,384]{1,0:T(8,128)(2,1)S(1)}, bf16[1024,384]{1,0:T(8,128)(2,1)}, u32[]{:S(2)}) copy-start(bf16[1024,384]{1,0:T(8,128)(2,1)} %feat_ref.1) | copy-start | bytes 2359300
